TPU v7x, 512 devices: a whole 4x4x16 slice. The times are simulated.
512 devices in a mesh: node: 32 (over y_hi, z), tp: 16 (over x, y_lo, core).
Axes of the slice: x: 4, y: 4 (y_hi: 2, y_lo: 2; y = y_hi * 2 + y_lo), z: 16, core: 2. Of those that a mesh axis runs over, the one named last changes fastest.
Arguments:
- weights: bfloat16 [32, 6912, 2560], P('node', 'tp'), may hold values from -6 to 6
- hidden: bfloat16 [32, 384, 6912], P('node', None, 'tp'), may hold values from -6 to 6
- cotangent: bfloat16 [32, 384, 2560], P('node', 'tp'), may hold values from -6 to 6
- hop_index: int32 [1], replicated, may hold values from 0 to 2
Outputs:
- layer_out: bfloat16 [32, 384, 2560], P('node', 'tp')
- new_weights: bfloat16 [32, 6912, 2560], P('node', 'tp')
Inputs may be any that keep to these rules, and one draw needn't show every extreme that they name: Node i averages with node i XOR 2^hop_index.
All inputs are finite; a program needn't handle non-finite values.
Results may differ from a plain program's by a relative error of at most 0.001.
Values may be sent and summed in bfloat16 or wider, within the bound.
No kernel may reach another device: no remote copies, remote signals or barrier semaphores. Data moves between devices by JAX's collectives and lax.ppermute only.
A program may use at most 64 MiB of HBM per device.

v0:
```python
from functools import partial

import jax
import jax.numpy as jnp
from jax import lax
from jax.sharding import PartitionSpec as P

FF = 6912


step_rate = 0.5
hop_levels = 3


def from_partner(value, axis, apart):
    return lax.ppermute(value, axis, [(i, i ^ 1 << apart) for i in range(lax.axis_size(axis))])


def trade_stepped(payload, bit_pos):
    return from_partner(payload, "node", bit_pos)


def with_partner(trader, payload, hop_index):
    branches = [partial(trader, bit_pos=hop_level) for hop_level in range(hop_levels)]
    return lax.switch(hop_index[0], branches, payload)


def per_device(weights, hidden, cotangent, hop_index):
    own_weights = weights[0]
    own_hidden = hidden[0]
    own_cotan = cotangent[0]
    multiplier = FF ** (-0.5)
    row_block = own_hidden
    layer_out = lax.psum_scatter(
        jnp.dot(row_block, own_weights, preferred_element_type=jnp.float32) * multiplier,
        "tp",
        scatter_dimension=0,
        tiled=True,
    ).astype(jnp.bfloat16)
    row_block = own_hidden
    gradient = (
        lax.dot_general(
            row_block,
            lax.all_gather(own_cotan, "tp", axis=0, tiled=True),
            (((0,), (0,)), ((), ())),
            preferred_element_type=jnp.float32,
        )
        * multiplier
    )
    stepped = own_weights.astype(jnp.float32) - step_rate * gradient
    far_stepped = with_partner(trade_stepped, stepped, hop_index)
    mean_stepped = (stepped + far_stepped) * 0.5
    new_weights = mean_stepped.astype(jnp.bfloat16)
    return (layer_out[None], new_weights[None])


def solution(mesh):
    placed = (P("node", "tp", None), P("node", None, "tp"), P("node", "tp", None), P())
    return jax.shard_map(
        per_device,
        mesh=mesh,
        in_specs=placed,
        out_specs=(P("node", "tp", None), P("node", "tp", None)),
        check_vma=False,
    )
```

profile of v0, /device:TPU:1, one launch (start us, length us, event | category | flops | bytes accessed | tf_op | source)
XLA Modules:
  0.0 463.9 jit_solution(12977453424492489634)
XLA Ops:
  7.2 0.0 copy-start
  7.2 0.0 all-gather.3.cloned.1.call-start
  7.2 0.7 all-gather.3.cloned.1.call-update
  7.9 0.0 copy-start.2
  7.9 0.0 reduce-scatter.2.cloned.1.call-start
  8.0 0.2 copy-done
  8.1 4.8 %convolution_multiply_fusion.1 = f32[384,2560]{1,0:T(8,128)} fusion(bf16[1,432,2560]{2,1,0:T(8,128)(2,1)} %param.7, bf16[1,384,432]{1,2,0:T(8,128)(2,1)S(1)} %copy-done), kind=kOutput, calls=%fused_computation.2 | convolution fusion | flops 850329600 | bytes 6475776 | tf_op jit(solution)/shard_map/dot_general | solution.py:35
  13.0 0.0 reduce-scatter.2.cloned.1.call-update
  13.7 43.7 %all-gather.3.cloned.1.call-done = bf16[1,384,2560]{2,1,0:T(8,128)(2,1)} async-done(((bf16[1,24,2560]{2,1,0:T(8,128)(2,1)}), bf16[1,384,2560]{2,1,0:T(8,128)(2,1)}) %all-gather.3.cloned.1.call-update) | async-done | bytes 1966096 | tf_op jit(solution)/shard_map/all_gather | solution.py:44
  57.3 0.0 copy-done.2
  57.3 2.9 fusion
  60.2 0.0 copy-start.1
  60.2 2.0 copy-done.1
  62.2 387.3 %conditional.1 = (f32[432,2560]{1,0:T(8,128)}) conditional(s32[]{:T(128)} %bitcast.4, f32[432,2560]{1,0:T(8,128)S(1)} %fusion, f32[432,2560]{1,0:T(8,128)S(1)} %fusion, f32[432,2560]{1,0:T(8,128)S(1)} %fusion), branch_computations={%region_1.0_spmd, %region_2.0_spmd, %region_3.0_spmd} | conditional | bytes 17694768 | solution.py:25
  62.2 7.4 %collective-permute-start.2 = (f32[432,2560]{1,0:T(8,128)S(1)}, f32[432,2560]{1,0:T(8,128)}, u32[]{:S(2)}, u32[]{:S(2)}) collective-permute-start(f32[432,2560]{1,0:T(8,128)S(1)} %param.2), channel_id=1, source_target_pairs={{0,64},{16,80},{32,96},{48,112},{64,0},{80,16},{96,32},{112,48},{1... | collective-permute-start | bytes 13271048 | tf_op jit(solution)/shard_map/cond/branch_2_fun/ppermute | solution.py:16
  69.6 379.9 %collective-permute-done.2 = f32[432,2560]{1,0:T(8,128)} collective-permute-done((f32[432,2560]{1,0:T(8,128)S(1)}, f32[432,2560]{1,0:T(8,128)}, u32[]{:S(2)}, u32[]{:S(2)}) %collective-permute-start.2) | collective-permute-done | bytes 4423712 | tf_op jit(solution)/shard_map/cond/branch_2_fun/ppermute | solution.py:16
  449.5 5.9 %fusion.1 = bf16[1,432,2560]{2,1,0:T(8,128)(2,1)} fusion(f32[432,2560]{1,0:T(8,128)} %copy-done.1, f32[432,2560]{1,0:T(8,128)} %get-tuple-element.9), kind=kLoop, calls=%fused_computation.4 | loop fusion | flops 3317760 | bytes 11059200 | tf_op jit(solution)/shard_map/broadcast_in_dim | solution.py:54
  455.5 0.0 reduce-scatter.2.cloned.1.call-done
  455.5 1.6 convert_bitcast_fusion
Async XLA Ops:
  7.2 1.0 copy-start
  7.2 50.2 %all-gather.3.cloned.1.call-start = ((), (), s32[]{:S(2)}) async-start(), calls=%async_computation.2 | async-start | bytes 2088960 | tf_op jit(solution)/shard_map/all_gather | solution.py:44
  7.9 49.4 %copy-start.2 = (bf16[1,432,2560]{2,1,0:T(8,128)(2,1)S(1)}, bf16[1,432,2560]{2,1,0:T(8,128)(2,1)}, u32[]{:S(2)}) copy-start(bf16[1,432,2560]{2,1,0:T(8,128)(2,1)} %param.7) | copy-start | bytes 6635524
  7.9 447.6 %reduce-scatter.2.cloned.1.call-start = ((), (), s32[]{:S(2)}) async-start(), calls=%async_computation.1 | async-start | bytes 4177920 | tf_op jit(solution)/shard_map/reduce_scatter | solution.py:34
  60.2 2.0 copy-start.1
  62.2 387.3 %collective-permute-start.2 = (f32[432,2560]{1,0:T(8,128)S(1)}, f32[432,2560]{1,0:T(8,128)}, u32[]{:S(2)}, u32[]{:S(2)}) collective-permute-start(f32[432,2560]{1,0:T(8,128)S(1)} %param.2), channel_id=1, source_target_pairs={{0,64},{16,80},{32,96},{48,112},{64,0},{80,16},{96,32},{112,48},{1... | collective-permute-start | bytes 13271048 | tf_op jit(solution)/shard_map/cond/branch_2_fun/ppermute | solution.py:16
Sparse Core Ops, SparseCore 0:
  10.2 47.1 all-gather.2
  60.2 73.4 reduce-scatter.1
where the time goes:
time: 464 us
  waiting for transfers between devices  424 us (91%)
  between operations  14.7 us (3%)
  matrix products  7.72 us (2%)
  other arithmetic  7.54 us (2%)
  starting transfers between devices  7.43 us (2%)
    ppermute x1, waiting for transfers between devices, from_partner(): lax.ppermute(value, axis, [(i, i ^ 1 << apart) for i in range(lax.axis_si...  380 us
    all_gather x1, waiting for transfers between devices, per_device(): lax.all_gather(own_cotan, 'tp', axis=0, tiled=True)  43.7 us
  transfers between devices with their start and end apart: 3, of which 2 were waited for; matrix products, arithmetic and copies ran while one was open for 3% of the time, Pallas kernels for 0%

commit v1 on v0

v1 whole, which is shorter than its diff:
```python
from functools import partial

import jax
import jax.numpy as jnp
from jax import lax
from jax.sharding import PartitionSpec as P

FF = 6912
STEP_RATE = 0.5
HOP_LEVELS = 3
SCALE = FF ** (-0.5)
CHUNKS = (168, 168, 96)


def trade(value, level):
    pairs = [(i, i ^ 1 << level) for i in range(lax.axis_size("node"))]
    return lax.ppermute(value, "node", pairs)


def step(level, weights, hidden, cotangent):
    tokens, rows = hidden.shape
    shard, width = cotangent.shape
    groups = tokens // shard
    far_cotangent = trade(cotangent, level)
    flipped = hidden.T
    far_flipped = trade(flipped, level)
    far_weights, first = [], 0
    for size in CHUNKS:
        far_weights.append(trade(weights[first : first + size], level))
        first += size
    both = lax.all_gather(
        jnp.concatenate([cotangent, far_cotangent], 0), "tp", axis=0, tiled=True
    )
    layer_out = lax.psum_scatter(
        jnp.dot(hidden, weights, preferred_element_type=jnp.float32) * SCALE,
        "tp",
        scatter_dimension=0,
        tiled=True,
    ).astype(jnp.bfloat16)
    paired = jnp.stack(
        [
            flipped.reshape(rows, groups, shard),
            far_flipped.reshape(rows, groups, shard),
        ],
        2,
    ).reshape(rows, 2 * tokens)
    means, first = [], 0
    for size, far in zip(CHUNKS, far_weights):
        here = slice(first, first + size)
        gradient = jnp.dot(paired[here], both, preferred_element_type=jnp.float32)
        total = weights[here].astype(jnp.float32) + far.astype(jnp.float32)
        means.append((0.5 * total - (0.5 * STEP_RATE * SCALE) * gradient).astype(jnp.bfloat16))
        first += size
    return layer_out, jnp.concatenate(means, 0)


def per_device(weights, hidden, cotangent, hop_index):
    branches = [partial(step, level) for level in range(HOP_LEVELS)]
    layer_out, new_weights = lax.switch(
        hop_index[0], branches, weights[0], hidden[0], cotangent[0]
    )
    return layer_out[None], new_weights[None]


def solution(mesh):
    placed = (P("node", "tp", None), P("node", None, "tp"), P("node", "tp", None), P())
    return jax.shard_map(
        per_device,
        mesh=mesh,
        in_specs=placed,
        out_specs=(P("node", "tp", None), P("node", "tp", None)),
        check_vma=False,
    )
```

time: 464 us -> 157 us (0.34)
  waiting for transfers between devices: 424 us -> 100 us
  starting transfers between devices: 7.43 us -> 18.4 us
    ppermute x1 -> x5, waiting for transfers between devices: 380 us -> 94.8 us  [trade(): return lax.ppermute(value, 'node', pairs)]
    all_gather x1, waiting for transfers between devices: 43.7 us -> 0.01 us  [step(): lax.all_gather(jnp.concatenate([cotangent, far_cotangent], 0), 'tp', axis...]
    ppermute x1 -> x5, starting transfers between devices: 7.35 us -> 18.3 us  [trade(): return lax.ppermute(value, 'node', pairs)]
    reduce_scatter x1, waiting for transfers between devices: 0.01 us -> 5.39 us  [step(): lax.psum_scatter(jnp.dot(hidden, weights, preferred_element_type=jnp.floa...]
    dot_general x2 -> x4, matrix products: 7.72 us -> 12.3 us  [the longest x3 7.65 us: step(): gradient = jnp.dot(paired[here], both, preferred_element_type=jnp.float32)]
  transfers between devices with their start and end apart: 3 -> 7, of which waited for: 2 -> 4; matrix products, arithmetic and copies ran while one was open for 3% -> 11% of each run, Pallas kernels for 0% -> 0%
where the time goes in v1:
time: 157 us; the launch traced here: 155 us
  waiting for transfers between devices  100 us (64%)
  starting transfers between devices  18.4 us (12%)
  between operations  14.7 us (9%)
  matrix products  12.3 us (8%)
  other arithmetic  6.57 us (4%)
  local copies, waits for them, and re-layouts  2.52 us (2%)
    ppermute x5, waiting for transfers between devices, trade(): return lax.ppermute(value, 'node', pairs)  94.8 us
    ppermute x5, starting transfers between devices, trade(): return lax.ppermute(value, 'node', pairs)  18.3 us
    dot_general x3, matrix products, step(): gradient = jnp.dot(paired[here], both, preferred_element_type=jnp.float32)  7.65 us
    reduce_scatter x1, waiting for transfers between devices, step(): lax.psum_scatter(jnp.dot(hidden, weights, preferred_element_type=jnp.floa...  5.39 us
    dot_general x1, matrix products, step(): jnp.dot(hidden, weights, preferred_element_type=jnp.float32) * SCALE  4.68 us
  transfers between devices with their start and end apart: 7, of which 4 were waited for; matrix products, arithmetic and copies ran while one was open for 11% of the time, Pallas kernels for 0%

profile of v1, /device:TPU:1, one launch (start us, length us, event | category | flops | bytes accessed | tf_op | source)
XLA Modules:
  0.0 154.9 jit_solution(7963114868599762762)
XLA Ops:
  7.2 1.1 copy.19
  9.0 139.1 %conditional.1 = (bf16[1,24,2560]{2,1,0:T(8,128)(2,1)}, bf16[1,432,2560]{2,1,0:T(8,128)(2,1)}) conditional(s32[]{:T(128)} %bitcast.30, (bf16[384,432]{1,0:T(8,128)(2,1)S(1)}, bf16[432,2560]{1,0:T(8,128)(2,1)}, bf16[24,2560]{1,0:T(8,128)(2,1)}) %tuple.59, (bf16[384,432]{1,0:T(8,128)(2,1)S(1)}, bf16[432,2560]{1,0:T(8,128)(2,1)}, ...), branch_computations={%region_0.0_spmd, %region_2.0_spmd, %region_4.0_spmd} | conditional | flops 2564505600 | bytes 99643800 | solution.py:59
  9.0 0.0 all-gather.6.cloned.1.call-start
  9.0 5.7 %collective-permute-start.7 = (bf16[24,2560]{1,0:T(8,128)(2,1)}, bf16[24,2560]{1,0:T(8,128)(2,1)S(1)}, u32[]{:S(2)}, u32[]{:S(2)}) collective-permute-start(bf16[24,2560]{1,0:T(8,128)(2,1)} %get-tuple-element.25), channel_id=1, source_target_pairs={{0,32},{16,48},{32,0},{48,16},{64,96},{80,112},{96,64},{112,80},{1... | collective-permute-start | bytes 368648 | tf_op jit(solution)/shard_map/cond/branch_1_fun/ppermute | solution.py:17
  14.8 2.5 %collective-permute-done.7 = bf16[24,2560]{1,0:T(8,128)(2,1)S(1)} collective-permute-done((bf16[24,2560]{1,0:T(8,128)(2,1)}, bf16[24,2560]{1,0:T(8,128)(2,1)S(1)}, u32[]{:S(2)}, u32[]{:S(2)}) %collective-permute-start.7) | collective-permute-done | bytes 122912 | tf_op jit(solution)/shard_map/cond/branch_1_fun/ppermute | solution.py:17
  17.2 1.6 %pad_maximum_fusion.2 = bf16[48,2560]{1,0:T(8,128)(2,1)} fusion(bf16[24,2560]{1,0:T(8,128)(2,1)S(1)} %collective-permute-done.7, bf16[24,2560]{1,0:T(8,128)(2,1)} %get-tuple-element.25), kind=kLoop, calls=%fused_computation.31 | loop fusion | flops 491520 | bytes 491520 | tf_op jit(solution)/shard_map/cond/branch_1_fun/concatenate | solution.py:32
  18.9 0.0 all-gather.6.cloned.1.call-update
  18.9 0.0 reduce-scatter.6.cloned.1.call-start
  18.9 4.7 %convolution_multiply_fusion.4 = f32[384,2560]{1,0:T(8,128)} fusion(bf16[384,432]{1,0:T(8,128)(2,1)S(1)} %get-tuple-element.23, bf16[432,2560]{1,0:T(8,128)(2,1)} %get-tuple-element.24), kind=kOutput, calls=%fused_computation.17 | convolution fusion | flops 850329600 | bytes 6475776 | tf_op jit(solution)/shard_map/cond/branch_1_fun/dot_general | solution.py:35
  23.6 0.0 copy-start.1
  23.6 0.0 reduce-scatter.6.cloned.1.call-update
  23.6 4.5 %collective-permute-start.6 = (bf16[432,384]{0,1:T(8,128)(2,1)S(1)}, bf16[432,384]{0,1:T(8,128)(2,1)S(1)}, u32[]{:S(2)}, u32[]{:S(2)}) collective-permute-start(bf16[432,384]{0,1:T(8,128)(2,1)S(1)} %bitcast.82), channel_id=1, source_target_pairs={{0,32},{16,48},{32,0},{48,16},{64,96},{80,112},{96,64},{112,80},{1... | collective-permute-start | bytes 995336 | tf_op jit(solution)/shard_map/cond/branch_1_fun/ppermute | solution.py:17
  28.1 0.0 copy-done.1
  28.1 1.0 fusion.7
  29.2 1.9 %collective-permute-start.8 = (bf16[168,2560]{1,0:T(8,128)(2,1)}, bf16[168,2560]{1,0:T(8,128)(2,1)}, u32[]{:S(2)}, u32[]{:S(2)}) collective-permute-start(bf16[168,2560]{1,0:T(8,128)(2,1)} %get-tuple-element.38), channel_id=1, source_target_pairs={{0,32},{16,48},{32,0},{48,16},{64,96},{80,112},{96,64},{112,80},{1... | collective-permute-start | bytes 2580488 | tf_op jit(solution)/shard_map/cond/branch_1_fun/ppermute | solution.py:17
  31.1 4.3 %collective-permute-start.9 = (bf16[96,2560]{1,0:T(8,128)(2,1)S(1)}, bf16[96,2560]{1,0:T(8,128)(2,1)}, u32[]{:S(2)}, u32[]{:S(2)}) collective-permute-start(bf16[96,2560]{1,0:T(8,128)(2,1)S(1)} %slice.78), channel_id=1, source_target_pairs={{0,32},{16,48},{32,0},{48,16},{64,96},{80,112},{96,64},{112,80},{1... | collective-permute-start | bytes 1474568 | tf_op jit(solution)/shard_map/cond/branch_1_fun/ppermute | solution.py:17
  35.4 1.9 %collective-permute-start.5 = (bf16[168,2560]{1,0:T(8,128)(2,1)S(1)}, bf16[168,2560]{1,0:T(8,128)(2,1)}, u32[]{:S(2)}, u32[]{:S(2)}) collective-permute-start(bf16[168,2560]{1,0:T(8,128)(2,1)S(1)} %get-tuple-element.37), channel_id=1, source_target_pairs={{0,32},{16,48},{32,0},{48,16},{64,96},{80,112},{96,64},{112,80},{1... | collective-permute-start | bytes 2580488 | tf_op jit(solution)/shard_map/cond/branch_1_fun/ppermute | solution.py:17
  37.3 0.0 collective-permute-done.6
  37.3 1.0 fusion.3
  38.4 0.8 pad_maximum_fusion.3
  39.2 79.8 %collective-permute-done.9 = bf16[96,2560]{1,0:T(8,128)(2,1)} collective-permute-done((bf16[96,2560]{1,0:T(8,128)(2,1)S(1)}, bf16[96,2560]{1,0:T(8,128)(2,1)}, u32[]{:S(2)}, u32[]{:S(2)}) %collective-permute-start.9) | collective-permute-done | bytes 491552 | tf_op jit(solution)/shard_map/cond/branch_1_fun/ppermute | solution.py:17
  119.0 3.3 %subtract_convert_fusion.5 = bf16[96,2560]{1,0:T(8,128)(2,1)S(1)} fusion(bf16[96,2560]{1,0:T(8,128)(2,1)} %collective-permute-done.9, bf16[96,768]{0,1:T(8,128)(2,1)} %bitcast.98, bf16[768,2560]{1,0:T(8,128)(2,1)} %all-gather.6.cloned.1.call-done, bf16[432,2560]{1,0:T(8,128)(2,1)S(1)} %copy-done.1), kind=kOutput, calls=%fused_computation.24 | convolution fusion | flops 379207680 | bytes 5554176 | tf_op jit(solution)/shard_map/cond/branch_1_fun/dot_general | solution.py:50
  122.3 0.0 collective-permute-done.8
  122.3 0.3 copy-done.4
  122.6 0.1 copy-done.10
  122.6 2.2 %subtract_convert_fusion.3 = bf16[168,2560]{1,0:T(8,128)(2,1)S(1)} fusion(bf16[168,2560]{1,0:T(8,128)(2,1)} %collective-permute-done.8, bf16[168,768]{0,1:T(8,128)(2,1)S(1)} %bitcast.104, bf16[768,2560]{1,0:T(8,128)(2,1)S(1)} %copy-done.4, bf16[432,2560]{1,0:T(8,128)(2,1)S(1)} %copy-done.1), kind=kOutput, calls=%fused_computation.22 | convolution fusion | flops 663613440 | bytes 6770688 | tf_op jit(solution)/shard_map/cond/branch_1_fun/dot_general | solution.py:50
  124.8 12.6 %collective-permute-done.5 = bf16[168,2560]{1,0:T(8,128)(2,1)} collective-permute-done((bf16[168,2560]{1,0:T(8,128)(2,1)S(1)}, bf16[168,2560]{1,0:T(8,128)(2,1)}, u32[]{:S(2)}, u32[]{:S(2)}) %collective-permute-start.5) | collective-permute-done | bytes 860192 | tf_op jit(solution)/shard_map/cond/branch_1_fun/ppermute | solution.py:17
  137.4 0.0 copy-done.7
  137.4 2.1 %subtract_convert_fusion.4 = bf16[168,2560]{1,0:T(8,128)(2,1)S(1)} fusion(bf16[168,2560]{1,0:T(8,128)(2,1)} %collective-permute-done.5, bf16[168,768]{0,1:T(8,128)(2,1)S(1)} %bitcast.101, bf16[768,2560]{1,0:T(8,128)(2,1)S(1)} %copy-done.4, bf16[432,2560]{1,0:T(8,128)(2,1)S(1)} %copy-done.1), kind=kOutput, calls=%fused_computation.23 | convolution fusion | flops 663613440 | bytes 6770688 | tf_op jit(solution)/shard_map/cond/branch_1_fun/dot_general | solution.py:50
  139.5 1.5 maximum_bitcast_fusion.1
  141.0 5.4 %reduce-scatter.6.cloned.1.call-done = f32[24,2560]{1,0:T(8,128)} async-done(((f32[384,2560]{1,0:T(8,128)}), f32[24,2560]{1,0:T(8,128)}) %reduce-scatter.6.cloned.1.call-update) | async-done | bytes 245776 | tf_op jit(solution)/shard_map/cond/branch_1_fun/reduce_scatter | solution.py:34
  146.4 1.6 %convert_bitcast_fusion.1 = bf16[1,24,2560]{2,1,0:T(8,128)(2,1)} fusion(f32[24,2560]{1,0:T(8,128)} %reduce-scatter.6.cloned.1.call-done), kind=kLoop, calls=%fused_computation.33 | loop fusion | flops 61440 | bytes 368640 | tf_op jit(solution)/shard_map/broadcast_in_dim | solution.py:62
  (5 shorter events, 0.0 us)
Async XLA Ops:
  9.0 110.0 %all-gather.6.cloned.1.call-start = ((), (), s32[]{:S(2)}) async-start(), calls=%async_computation.6 | async-start | bytes 4177920 | tf_op jit(solution)/shard_map/cond/branch_1_fun/all_gather | solution.py:31
  9.0 8.2 %collective-permute-start.7 = (bf16[24,2560]{1,0:T(8,128)(2,1)}, bf16[24,2560]{1,0:T(8,128)(2,1)S(1)}, u32[]{:S(2)}, u32[]{:S(2)}) collective-permute-start(bf16[24,2560]{1,0:T(8,128)(2,1)} %get-tuple-element.25), channel_id=1, source_target_pairs={{0,32},{16,48},{32,0},{48,16},{64,96},{80,112},{96,64},{112,80},{1... | collective-permute-start | bytes 368648 | tf_op jit(solution)/shard_map/cond/branch_1_fun/ppermute | solution.py:17
  18.9 127.5 %reduce-scatter.6.cloned.1.call-start = ((), (), s32[]{:S(2)}) async-start(), calls=%async_computation.5 | async-start | bytes 4177920 | tf_op jit(solution)/shard_map/cond/branch_1_fun/reduce_scatter | solution.py:34
  23.6 4.5 %copy-start.1 = (bf16[432,2560]{1,0:T(8,128)(2,1)S(1)}, bf16[432,2560]{1,0:T(8,128)(2,1)}, u32[]{:S(2)}) copy-start(bf16[432,2560]{1,0:T(8,128)(2,1)} %get-tuple-element.24) | copy-start | bytes 6635524 | tf_op jit(solution)/shard_map/cond
  23.6 13.7 %collective-permute-start.6 = (bf16[432,384]{0,1:T(8,128)(2,1)S(1)}, bf16[432,384]{0,1:T(8,128)(2,1)S(1)}, u32[]{:S(2)}, u32[]{:S(2)}) collective-permute-start(bf16[432,384]{0,1:T(8,128)(2,1)S(1)} %bitcast.82), channel_id=1, source_target_pairs={{0,32},{16,48},{32,0},{48,16},{64,96},{80,112},{96,64},{112,80},{1... | collective-permute-start | bytes 995336 | tf_op jit(solution)/shard_map/cond/branch_1_fun/ppermute | solution.py:17
  29.2 93.1 %collective-permute-start.8 = (bf16[168,2560]{1,0:T(8,128)(2,1)}, bf16[168,2560]{1,0:T(8,128)(2,1)}, u32[]{:S(2)}, u32[]{:S(2)}) collective-permute-start(bf16[168,2560]{1,0:T(8,128)(2,1)} %get-tuple-element.38), channel_id=1, source_target_pairs={{0,32},{16,48},{32,0},{48,16},{64,96},{80,112},{96,64},{112,80},{1... | collective-permute-start | bytes 2580488 | tf_op jit(solution)/shard_map/cond/branch_1_fun/ppermute | solution.py:17
  31.1 87.8 %collective-permute-start.9 = (bf16[96,2560]{1,0:T(8,128)(2,1)S(1)}, bf16[96,2560]{1,0:T(8,128)(2,1)}, u32[]{:S(2)}, u32[]{:S(2)}) collective-permute-start(bf16[96,2560]{1,0:T(8,128)(2,1)S(1)} %slice.78), channel_id=1, source_target_pairs={{0,32},{16,48},{32,0},{48,16},{64,96},{80,112},{96,64},{112,80},{1... | collective-permute-start | bytes 1474568 | tf_op jit(solution)/shard_map/cond/branch_1_fun/ppermute | solution.py:17
  35.4 102.0 %collective-permute-start.5 = (bf16[168,2560]{1,0:T(8,128)(2,1)S(1)}, bf16[168,2560]{1,0:T(8,128)(2,1)}, u32[]{:S(2)}, u32[]{:S(2)}) collective-permute-start(bf16[168,2560]{1,0:T(8,128)(2,1)S(1)} %get-tuple-element.37), channel_id=1, source_target_pairs={{0,32},{16,48},{32,0},{48,16},{64,96},{80,112},{96,64},{112,80},{1... | collective-permute-start | bytes 2580488 | tf_op jit(solution)/shard_map/cond/branch_1_fun/ppermute | solution.py:17
  118.9 3.6 %copy-start.4 = (bf16[768,2560]{1,0:T(8,128)(2,1)S(1)}, bf16[768,2560]{1,0:T(8,128)(2,1)}, u32[]{:S(2)}) copy-start(bf16[768,2560]{1,0:T(8,128)(2,1)} %all-gather.6.cloned.1.call-done) | copy-start | bytes 11796484 | tf_op jit(solution)/shard_map/cond
  119.0 3.7 %copy-start.10 = (bf16[168,16,2,24]{0,3,2,1:T(8,128)(2,1)S(1)}, bf16[168,16,2,24]{0,3,2,1:T(8,128)(2,1)}, u32[]{:S(2)}) copy-start(bf16[168,16,2,24]{0,3,2,1:T(8,128)(2,1)} %get-tuple-element.40) | copy-start | bytes 774148 | tf_op jit(solution)/shard_map/cond
  122.6 14.8 %copy-start.7 = (bf16[168,16,2,24]{0,3,2,1:T(8,128)(2,1)S(1)}, bf16[168,16,2,24]{0,3,2,1:T(8,128)(2,1)}, u32[]{:S(2)}) copy-start(bf16[168,16,2,24]{0,3,2,1:T(8,128)(2,1)} %get-tuple-element.39) | copy-start | bytes 774148 | tf_op jit(solution)/shard_map/cond
Sparse Core Ops, SparseCore 0:
  19.0 52.6 all-gather.5
  74.8 71.5 reduce-scatter.5

commit v2 on v1

v2 whole, which is shorter than its diff:
```python
from functools import partial

import jax
import jax.numpy as jnp
from jax import lax
from jax.experimental import pallas as pl
from jax.sharding import PartitionSpec as P

FF = 6912
STEP_RATE = 0.5
HOP_LEVELS = 3
SCALE = FF ** (-0.5)
CORES = 2
PLANS = {1: (112, (56, 56, 48), 1), 2: (0, (56, 56, 56, 48), 2)}


def after(value, *others):
    return lax.optimization_barrier((value, *others))[0]


def trade(value, level):
    pairs = [(i, i ^ 1 << level) for i in range(lax.axis_size("node"))]
    return lax.ppermute(value, "node", pairs)


def swap_cores(value):
    return lax.ppermute(value, "tp", [(i, i ^ 1) for i in range(lax.axis_size("tp"))])


def between_chips(blocks):
    chips = blocks.shape[0]
    same_core = [[CORES * i + j for i in range(chips)] for j in range(CORES)]
    return lax.all_to_all(blocks, "tp", 0, 0, axis_index_groups=same_core, tiled=True)


def chip_output(weights, hidden):
    tokens, rows = hidden.shape
    members = lax.axis_size("tp")
    chips, shard = members // CORES, tokens // members
    core = lax.rem(lax.axis_index("tp"), CORES)
    panel = hidden.reshape(chips, CORES, shard, rows)

    def partial_of(owner):
        chosen = lax.dynamic_index_in_dim(panel, owner, 1, keepdims=False)
        return SCALE * jnp.dot(
            chosen.reshape(chips * shard, rows), weights, preferred_element_type=jnp.float32
        )

    far = swap_cores(partial_of(1 - core))
    return (partial_of(core) + far).reshape(chips, shard, -1)


def interleave(near, far, members):
    rows, tokens = near.shape
    blocks = (rows, members, tokens // members)
    return jnp.stack([near.reshape(blocks), far.reshape(blocks)], 2).reshape(rows, 2 * tokens)


def arrived(value, *others, ahead=10**12):
    return pl.pallas_call(
        lambda *refs: None,
        in_specs=[pl.BlockSpec(memory_space=pl.ANY)] * (1 + len(others)),
        out_specs=pl.BlockSpec(memory_space=pl.ANY),
        out_shape=jax.ShapeDtypeStruct(value.shape, value.dtype),
        input_output_aliases={0: 0},
        cost_estimate=pl.CostEstimate(flops=ahead, bytes_accessed=0, transcendentals=0),
    )(value, *others)


def averaged(near, far, gradient):
    total = near.astype(jnp.float32) + far.astype(jnp.float32)
    return (0.5 * total - (0.5 * STEP_RATE * SCALE) * gradient).astype(jnp.bfloat16)


def pieces_of(sizes):
    first = 0
    for size in sizes:
        yield first, size
        first += size


def whole_step(level, weights, hidden, cotangent):
    tokens, rows = hidden.shape
    members = lax.axis_size("tp")
    far_cotangent = trade(cotangent, level)
    far_hidden = trade(hidden, level)
    far_weights = trade(weights, level)
    shards = jnp.concatenate([cotangent, far_cotangent], 0)
    both = lax.all_gather(shards, "tp", axis=0, tiled=True)
    chip_sum = chip_output(weights, hidden)
    layer_out = between_chips(chip_sum).sum(0).astype(jnp.bfloat16)
    both = arrived(both, far_weights, layer_out, ahead=0)
    blocks = (members, tokens // members, rows)
    panel = jnp.stack([hidden.reshape(blocks), far_hidden.reshape(blocks)], 1)
    gradient = lax.dot_general(
        panel.reshape(2 * tokens, rows),
        both,
        (((0,), (0,)), ((), ())),
        preferred_element_type=jnp.float32,
    )
    return layer_out, averaged(weights, far_weights, gradient)


def mixed_step(level, weights, hidden, cotangent):
    members = lax.axis_size("tp")
    shared, pieces, forward_by = PLANS[level]
    half = (weights.shape[0] - shared) // 2
    upper = (lax.axis_index("node") >> level) & 1
    mine, other = shared + half * upper, shared + half * (1 - upper)
    far_cotangent = trade(cotangent, level)
    shards = jnp.concatenate([cotangent, far_cotangent], 0)
    flipped = hidden.T

    def with_shared(first):
        if not shared:
            return lax.dynamic_slice_in_dim(flipped, first, half, 0)
        return jnp.concatenate(
            [flipped[:shared], lax.dynamic_slice_in_dim(flipped, first, half, 0)], 0
        )

    far_flipped = trade(after(with_shared(other), shards), level)
    far_weights = [
        trade(after(lax.dynamic_slice_in_dim(weights, other + a, n, 0), shards), level)
        for a, n in pieces_of(pieces)
    ]
    if shared:
        far_shared = trade(after(weights[:shared], shards), level)
    both = lax.all_gather(shards, "tp", axis=0, tiled=True)
    chip_sum = chip_output(weights, after(hidden, both))
    layer_out = between_chips(chip_sum).sum(0).astype(jnp.bfloat16)
    paired = interleave(with_shared(mine), far_flipped, members)
    gradient = jnp.dot(paired, both, preferred_element_type=jnp.float32)
    new_weights = jnp.zeros_like(weights)
    returned, order = [], []
    for k, ((a, n), far) in enumerate(zip(pieces_of(pieces), far_weights)):
        if k == forward_by:
            order.append(chip_sum)
        near = lax.dynamic_slice_in_dim(weights, mine + a, n, 0)
        mean = averaged(near, arrived(far, *order), gradient[shared + a : shared + a + n])
        order = [mean]
        returned.append(trade(mean, level))
        new_weights = lax.dynamic_update_slice_in_dim(new_weights, mean, mine + a, 0)
    if shared:
        far_shared = arrived(far_shared, *order)
        mean = averaged(weights[:shared], far_shared, gradient[:shared])
        new_weights = lax.dynamic_update_slice_in_dim(new_weights, mean, 0, 0)
    returned[-1] = arrived(returned[-1], layer_out, ahead=0)
    for (a, n), mean in zip(pieces_of(pieces), returned):
        new_weights = lax.dynamic_update_slice_in_dim(new_weights, mean, other + a, 0)
    return layer_out, new_weights


def per_device(weights, hidden, cotangent, hop_index):
    branches = [
        partial(mixed_step if level in PLANS else whole_step, level) for level in range(HOP_LEVELS)
    ]
    layer_out, new_weights = lax.switch(
        hop_index[0], branches, weights[0], hidden[0], cotangent[0]
    )
    return layer_out[None], new_weights[None]


def solution(mesh):
    placed = (P("node", "tp", None), P("node", None, "tp"), P("node", "tp", None), P())
    return jax.shard_map(
        per_device,
        mesh=mesh,
        in_specs=placed,
        out_specs=(P("node", "tp", None), P("node", "tp", None)),
        check_vma=False,
    )
```

time: 157 us -> 147 us (0.936)
  the two profiles are of different devices: /device:TPU:1 before, /device:TPU:24 now
where the time goes in v2:
time: 147 us; the launch traced here: 146 us
  waiting for transfers between devices  56 us (38%)
  starting transfers between devices  37.1 us (25%)
  local copies, waits for them, and re-layouts  17.2 us (12%)
  between operations  14.7 us (10%)
  other arithmetic  11.3 us (8%)
  matrix products  9.05 us (6%)
    ppermute x9, waiting for transfers between devices, trade(): return lax.ppermute(value, 'node', pairs)  56 us
    ppermute x9, starting transfers between devices, trade(): return lax.ppermute(value, 'node', pairs)  29.4 us
    all_to_all x1, starting transfers between devices, between_chips(): lax.all_to_all(blocks, 'tp', 0, 0, axis_index_groups=same_core, tiled=True)  5.75 us
    dot_general x2, matrix products, partial_of(): jnp.dot(chosen.reshape(chips * shard, rows), weights, preferred_element_t...  5.62 us
    another operation x17, local copies, waits for them, and re-layouts  5.19 us
    dynamic_update_slice x3, other arithmetic, mixed_step(): lax.dynamic_update_slice_in_dim(new_weights, mean, mine + a, 0)  5.19 us
    dynamic_update_slice x3, local copies, waits for them, and re-layouts, mixed_step(): lax.dynamic_update_slice_in_dim(new_weights, mean, other + a, 0)  5.03 us
    dot_general x1, matrix products, mixed_step(): gradient = jnp.dot(paired, both, preferred_element_type=jnp.float32)  3.43 us
  transfers between devices with their start and end apart: 12, of which 5 were waited for; matrix products, arithmetic and copies ran while one was open for 21% of the time, Pallas kernels for 0%

profile of v2, /device:TPU:24, one launch (start us, length us, event | category | flops | bytes accessed | tf_op | source)
XLA Modules:
  0.0 145.7 jit_solution(15305088222379589315)
XLA Ops:
  7.8 1.1 copy.25
  9.0 129.9 %conditional.2 = (bf16[24,2560]{1,0:T(8,128)(2,1)}, bf16[1,432,2560]{2,1,0:T(8,128)(2,1)}) conditional(s32[]{:T(128)} %bitcast.48, (bf16[1,384,432]{1,2,0:T(8,128)(2,1)}, bf16[432,2560]{1,0:T(8,128)(2,1)}, bf16[384,432]{1,0:T(8,128)(2,1)S(1)}, bf16[24,2560]{1,0:T(8,128)(2,1)}) %tuple.75, (bf16[24,2560]{1,0:T(8,128)(2,1)}, ...), branch_computations={%region_0.2_spmd, %region_2.4_spmd, %region_4.6_spmd} | conditional | flops 4001926479872 | bytes 122447392
  9.1 5.3 %collective-permute-start.4 = (bf16[24,2560]{1,0:T(8,128)(2,1)}, bf16[24,2560]{1,0:T(8,128)(2,1)S(1)}, u32[]{:S(2)}, u32[]{:S(2)}) collective-permute-start(bf16[24,2560]{1,0:T(8,128)(2,1)} %get-tuple-element.29), channel_id=1, source_target_pairs={{0,32},{16,48},{32,0},{48,16},{64,96},{80,112},{96,64},{112,80},{1... | collective-permute-start | bytes 368648 | tf_op jit(solution)/shard_map/cond/branch_1_fun/ppermute | solution.py:23
  15.3 5.2 %collective-permute-done.4 = bf16[24,2560]{1,0:T(8,128)(2,1)S(1)} collective-permute-done((bf16[24,2560]{1,0:T(8,128)(2,1)}, bf16[24,2560]{1,0:T(8,128)(2,1)S(1)}, u32[]{:S(2)}, u32[]{:S(2)}) %collective-permute-start.4) | collective-permute-done | bytes 122912 | tf_op jit(solution)/shard_map/cond/branch_1_fun/ppermute | solution.py:23
  21.3 1.9 %slice.26 = bf16[112,2560]{1,0:T(8,128)(2,1)} slice(bf16[432,2560]{1,0:T(8,128)(2,1)} %get-tuple-element.31), slice={[0:112], [0:2560]} | slice | bytes 1146880 | tf_op jit(solution)/shard_map/cond/branch_1_fun/slice | solution.py:145
  24.5 2.0 %collective-permute-start.7 = (bf16[272,384]{0,1:T(8,128)(2,1)S(1)}, bf16[272,384]{0,1:T(8,128)(2,1)S(1)}, u32[]{:S(2)}, u32[]{:S(2)}) collective-permute-start(bf16[272,384]{0,1:T(8,128)(2,1)S(1)} %get-tuple-element.33), channel_id=1, source_target_pairs={{0,32},{16,48},{32,0},{48,16},{64,96},{80,112},{96,64},{112,80},{1... | collective-permute-start | bytes 626696 | tf_op jit(solution)/shard_map/cond/branch_1_fun/ppermute | solution.py:23
  27.2 4.7 %collective-permute-start.9 = (bf16[48,2560]{1,0:T(8,128)(2,1)}, bf16[48,2560]{1,0:T(8,128)(2,1)}, u32[]{:S(2)}, u32[]{:S(2)}) collective-permute-start(bf16[48,2560]{1,0:T(8,128)(2,1)} %constant_dynamic-slice_fusion.2), channel_id=1, source_target_pairs={{0,32},{16,48},{32,0},{48,16},{64,96},{80,112},{96,64},{112,80},{1... | collective-permute-start | bytes 737288 | tf_op jit(solution)/shard_map/cond/branch_1_fun/ppermute | solution.py:23
  31.9 2.0 %collective-permute-start.6 = (bf16[56,2560]{1,0:T(8,128)(2,1)S(1)}, bf16[56,2560]{1,0:T(8,128)(2,1)S(1)}, u32[]{:S(2)}, u32[]{:S(2)}) collective-permute-start(bf16[56,2560]{1,0:T(8,128)(2,1)S(1)} %get-tuple-element.32), channel_id=1, source_target_pairs={{0,32},{16,48},{32,0},{48,16},{64,96},{80,112},{96,64},{112,80},{1... | collective-permute-start | bytes 860168 | tf_op jit(solution)/shard_map/cond/branch_1_fun/ppermute | solution.py:23
  34.0 4.8 %collective-permute-start.8 = (bf16[56,2560]{1,0:T(8,128)(2,1)}, bf16[56,2560]{1,0:T(8,128)(2,1)}, u32[]{:S(2)}, u32[]{:S(2)}) collective-permute-start(bf16[56,2560]{1,0:T(8,128)(2,1)} %get-tuple-element.34), channel_id=1, source_target_pairs={{0,32},{16,48},{32,0},{48,16},{64,96},{80,112},{96,64},{112,80},{1... | collective-permute-start | bytes 860168 | tf_op jit(solution)/shard_map/cond/branch_1_fun/ppermute | solution.py:23
  38.7 2.0 %collective-permute-start.10 = (bf16[112,2560]{1,0:T(8,128)(2,1)}, bf16[112,2560]{1,0:T(8,128)(2,1)}, u32[]{:S(2)}, u32[]{:S(2)}) collective-permute-start(bf16[112,2560]{1,0:T(8,128)(2,1)} %slice.26), channel_id=1, source_target_pairs={{0,32},{16,48},{32,0},{48,16},{64,96},{80,112},{96,64},{112,80},{1... | collective-permute-start | bytes 1720328 | tf_op jit(solution)/shard_map/cond/branch_1_fun/ppermute | solution.py:23
  40.7 32.6 %collective-permute-done.7 = bf16[272,384]{0,1:T(8,128)(2,1)S(1)} collective-permute-done((bf16[272,384]{0,1:T(8,128)(2,1)S(1)}, bf16[272,384]{0,1:T(8,128)(2,1)S(1)}, u32[]{:S(2)}, u32[]{:S(2)}) %collective-permute-start.7) | collective-permute-done | bytes 208928 | tf_op jit(solution)/shard_map/cond/branch_1_fun/ppermute | solution.py:23
  75.0 2.1 %convolution_multiply_fusion.3 = f32[192,2560]{1,0:T(8,128)} fusion(bf16[192,432]{1,0:T(8,128)(2,1)S(1)} %bitcast.125, bf16[432,2560]{1,0:T(8,128)(2,1)S(1)} %copy-done.1), kind=kOutput, calls=%fused_computation.10 | convolution fusion | flops 425164800 | bytes 4343808 | tf_op jit(solution)/shard_map/cond/branch_1_fun/dot_general | solution.py:45
  77.1 1.9 %collective-permute-start.5 = (f32[192,2560]{1,0:T(8,128)}, f32[192,2560]{1,0:T(8,128)}, u32[]{:S(2)}, u32[]{:S(2)}) collective-permute-start(f32[192,2560]{1,0:T(8,128)} %convolution_multiply_fusion.3), channel_id=1, source_target_pairs={{0,1},{1,0},{2,3},{3,2},{4,5},{5,4},{6,7},{7,6},{8,9},{9,8},{10,11... | collective-permute-start | bytes 5898248 | tf_op jit(solution)/shard_map/cond/branch_1_fun/ppermute | solution.py:27
  79.0 5.8 %collective-permute-done.6.refs_0_ = bf16[56,2560]{1,0:T(8,128)(2,1)S(1)} collective-permute-done((bf16[56,2560]{1,0:T(8,128)(2,1)S(1)}, bf16[56,2560]{1,0:T(8,128)(2,1)S(1)}, u32[]{:S(2)}, u32[]{:S(2)}) %collective-permute-start.6) | collective-permute-done | bytes 286752 | tf_op jit(solution)/shard_map/cond/branch_1_fun/ppermute | solution.py:23
  85.5 1.1 copy-done.10
  86.6 3.4 %fusion.29 = f32[272,2560]{1,0:T(8,128)S(1)} fusion(bf16[272,768]{0,1:T(8,128)(2,1)S(1)} %bitcast.115, bf16[768,2560]{1,0:T(8,128)(2,1)} %all-gather.6.cloned.1.call-done), kind=kOutput, calls=%fused_computation.80 | convolution fusion | flops 1069547520 | bytes 7135232 | tf_op jit(solution)/shard_map/cond/branch_1_fun/dot_general | solution.py:132
  90.0 1.5 %broadcast_in_dim.7 = bf16[1,432,2560]{2,1,0:T(8,128)(2,1)} broadcast(bf16[]{:T(256)} %constant.126.clone), dimensions={} | broadcast | bytes 2211842 | tf_op jit(solution)/shard_map/broadcast_in_dim | solution.py:160
  91.5 1.8 %copy-done.2 = bf16[432,2560]{1,0:T(8,128)(2,1)S(1)} copy-done((bf16[432,2560]{1,0:T(8,128)(2,1)S(1)}, bf16[432,2560]{1,0:T(8,128)(2,1)}, u32[]{:S(2)}) %copy-start.2) | copy-done | bytes 2211864 | tf_op jit(solution)/shard_map/conditional
  94.2 1.9 %collective-permute-start.11 = (bf16[56,2560]{1,0:T(8,128)(2,1)}, bf16[56,2560]{1,0:T(8,128)(2,1)}, u32[]{:S(2)}, u32[]{:S(2)}) collective-permute-start(bf16[56,2560]{1,0:T(8,128)(2,1)} %get-tuple-element.65.refs_1_), channel_id=1, source_target_pairs={{0,32},{16,48},{32,0},{48,16},{64,96},{80,112},{96,64},{112,80},{1... | collective-permute-start | bytes 860168 | tf_op jit(solution)/shard_map/cond/branch_1_fun/ppermute | solution.py:23
  96.2 3.6 %fusion.2 = f32[192,2560]{1,0:T(8,128)} fusion(f32[192,2560]{1,0:T(8,128)} %collective-permute-done.5, bf16[192,432]{1,0:T(8,128)(2,1)S(1)} %bitcast.122, bf16[432,2560]{1,0:T(8,128)(2,1)S(1)} %copy-done.2), kind=kOutput, calls=%fused_computation.12 | convolution fusion | flops 425656320 | bytes 6309888 | tf_op jit(solution)/shard_map/cond/branch_1_fun/dot_general | solution.py:45
  99.7 5.8 %all-to-all-start.1 = ((f32[8,24,2560]{2,1,0:T(8,128)}), f32[8,24,2560]{2,1,0:T(8,128)}, u32[]{:S(2)}, u32[]{:S(2)}) async-start(f32[8,24,2560]{2,1,0:T(8,128)} %bitcast.13.refs_2_), calls=%async_computation.1 | async-start | bytes 3932160 | tf_op jit(solution)/shard_map/cond/branch_1_fun/all_to_all | solution.py:33
  105.5 2.1 %bitcast_dynamic-update-slice_fusion.2 = (bf16[1,432,2560]{2,1,0:T(8,128)(2,1)}, bf16[56,2560]{1,0:T(8,128)(2,1)}) fusion(bf16[1,432,2560]{2,1,0:T(8,128)(2,1)} %get-tuple-element.64, s32[]{:T(128)S(6)} %select_n.47, f32[272,2560]{1,0:T(8,128)} %copy-done.5, bf16[56,2560]{1,0:T(8,128)(2,1)} %branch_1_fun.6, bf16[432,2560]{1,0:T(8,128)(2,1)} %get-tuple-element.31), kind=kLoop, calls=%fused_computation.32 | loop fusion | flops 1003520 | bytes 1720324 | tf_op jit(solution)/shard_map/cond/branch_1_fun/dynamic_update_slice | solution.py:142
  107.6 4.8 %collective-permute-start.12 = (bf16[56,2560]{1,0:T(8,128)(2,1)}, bf16[56,2560]{1,0:T(8,128)(2,1)}, u32[]{:S(2)}, u32[]{:S(2)}) collective-permute-start(bf16[56,2560]{1,0:T(8,128)(2,1)} %get-tuple-element.63.refs_1_), channel_id=1, source_target_pairs={{0,32},{16,48},{32,0},{48,16},{64,96},{80,112},{96,64},{112,80},{1... | collective-permute-start | bytes 860168 | tf_op jit(solution)/shard_map/cond/branch_1_fun/ppermute | solution.py:23
  112.5 2.1 %bitcast_dynamic-update-slice_fusion.5 = (bf16[1,432,2560]{2,1,0:T(8,128)(2,1)}, bf16[48,2560]{1,0:T(8,128)(2,1)}) fusion(bf16[1,432,2560]{2,1,0:T(8,128)(2,1)} %get-tuple-element.62, s32[]{:T(128)S(6)} %select_n.67, f32[272,2560]{1,0:T(8,128)} %copy-done.5, bf16[48,2560]{1,0:T(8,128)(2,1)} %branch_1_fun.7, bf16[432,2560]{1,0:T(8,128)(2,1)} %get-tuple-element.31), kind=kLoop, calls=%fused_computation.35 | loop fusion | flops 860160 | bytes 1474564 | tf_op jit(solution)/shard_map/cond/branch_1_fun/dynamic_update_slice | solution.py:142
  114.6 1.9 %collective-permute-start.13 = (bf16[48,2560]{1,0:T(8,128)(2,1)}, bf16[48,2560]{1,0:T(8,128)(2,1)}, u32[]{:S(2)}, u32[]{:S(2)}) collective-permute-start(bf16[48,2560]{1,0:T(8,128)(2,1)} %get-tuple-element.61.refs_1_), channel_id=1, source_target_pairs={{0,32},{16,48},{32,0},{48,16},{64,96},{80,112},{96,64},{112,80},{1... | collective-permute-start | bytes 737288 | tf_op jit(solution)/shard_map/cond/branch_1_fun/ppermute | solution.py:23
  116.5 2.6 %fusion.6 = bf16[1,432,2560]{2,1,0:T(8,128)(2,1)} fusion(bf16[1,432,2560]{2,1,0:T(8,128)(2,1)} %get-tuple-element.60, f32[272,2560]{1,0:T(8,128)} %copy-done.5, bf16[112,2560]{1,0:T(8,128)(2,1)} %branch_1_fun.8, bf16[432,2560]{1,0:T(8,128)(2,1)} %get-tuple-element.31), kind=kLoop, calls=%fused_computation.18 | loop fusion | flops 2007040 | bytes 2867200 | tf_op jit(solution)/shard_map/cond/branch_1_fun/dynamic_update_slice | solution.py:146
  119.2 7.8 %collective-permute-done.11 = bf16[56,2560]{1,0:T(8,128)(2,1)} collective-permute-done((bf16[56,2560]{1,0:T(8,128)(2,1)}, bf16[56,2560]{1,0:T(8,128)(2,1)}, u32[]{:S(2)}, u32[]{:S(2)}) %collective-permute-start.11) | collective-permute-done | bytes 286752 | tf_op jit(solution)/shard_map/cond/branch_1_fun/ppermute | solution.py:23
  127.0 1.7 %bitcast_dynamic-update-slice_fusion.1 = bf16[1,432,2560]{2,1,0:T(8,128)(2,1)} fusion(bf16[1,432,2560]{2,1,0:T(8,128)(2,1)} %fusion.6, s32[]{:T(128)S(6)} %select_n.46, bf16[56,2560]{1,0:T(8,128)(2,1)} %collective-permute-done.11), kind=kLoop, calls=%fused_computation.31 | loop fusion | bytes 573444 | tf_op jit(solution)/shard_map/cond/branch_1_fun/dynamic_update_slice | solution.py:149
  128.7 4.5 %collective-permute-done.12 = bf16[56,2560]{1,0:T(8,128)(2,1)} collective-permute-done((bf16[56,2560]{1,0:T(8,128)(2,1)}, bf16[56,2560]{1,0:T(8,128)(2,1)}, u32[]{:S(2)}, u32[]{:S(2)}) %collective-permute-start.12) | collective-permute-done | bytes 286752 | tf_op jit(solution)/shard_map/cond/branch_1_fun/ppermute | solution.py:23
  133.1 1.7 %bitcast_dynamic-update-slice_fusion = bf16[1,432,2560]{2,1,0:T(8,128)(2,1)} fusion(bf16[1,432,2560]{2,1,0:T(8,128)(2,1)} %bitcast_dynamic-update-slice_fusion.1, s32[]{:T(128)S(6)} %select_n.66, bf16[56,2560]{1,0:T(8,128)(2,1)} %collective-permute-done.12), kind=kLoop, calls=%fused_computation.30 | loop fusion | bytes 573444 | tf_op jit(solution)/shard_map/cond/branch_1_fun/dynamic_update_slice | solution.py:149
  134.8 2.3 %reduce_sum.25.refs_1_ = bf16[24,2560]{1,0:T(8,128)(2,1)} reduce(f32[8,24,2560]{2,1,0:T(8,128)} %all-to-all-done.1, f32[]{:T(128)} %constant.125.clone), dimensions={0}, to_apply=%region_3.3 | reduce | flops 430080 | bytes 2088964 | tf_op jit(solution)/shard_map/cond/branch_1_fun/reduce_sum | solution.py:130
  137.2 1.7 %bitcast_dynamic-update-slice_fusion.4 = bf16[1,432,2560]{2,1,0:T(8,128)(2,1)} fusion(bf16[1,432,2560]{2,1,0:T(8,128)(2,1)} %bitcast_dynamic-update-slice_fusion, s32[]{:T(128)S(6)} %select_n.68, bf16[48,2560]{1,0:T(8,128)(2,1)} %branch_1_fun.9), kind=kLoop, calls=%fused_computation.34 | loop fusion | bytes 491524 | tf_op jit(solution)/shard_map/cond/branch_1_fun/dynamic_update_slice | solution.py:149
  (38 shorter events, 7.0 us)
Async XLA Ops:
  9.0 14.7 %copy-start.1 = (bf16[432,2560]{1,0:T(8,128)(2,1)S(1)}, bf16[432,2560]{1,0:T(8,128)(2,1)}, u32[]{:S(2)}) copy-start(bf16[432,2560]{1,0:T(8,128)(2,1)} %get-tuple-element.31) | copy-start | bytes 6635524 | tf_op jit(solution)/shard_map/conditional
  9.0 65.3 %all-gather.6.cloned.1.call-start = ((), (), s32[]{:S(2)}) async-start(), calls=%async_computation.4 | async-start | bytes 4177920 | tf_op jit(solution)/shard_map/cond/branch_1_fun/all_gather | solution.py:128
  9.1 11.5 %collective-permute-start.4 = (bf16[24,2560]{1,0:T(8,128)(2,1)}, bf16[24,2560]{1,0:T(8,128)(2,1)S(1)}, u32[]{:S(2)}, u32[]{:S(2)}) collective-permute-start(bf16[24,2560]{1,0:T(8,128)(2,1)} %get-tuple-element.29), channel_id=1, source_target_pairs={{0,32},{16,48},{32,0},{48,16},{64,96},{80,112},{96,64},{112,80},{1... | collective-permute-start | bytes 368648 | tf_op jit(solution)/shard_map/cond/branch_1_fun/ppermute | solution.py:23
  20.5 0.7 copy-start.17
  24.5 48.9 %collective-permute-start.7 = (bf16[272,384]{0,1:T(8,128)(2,1)S(1)}, bf16[272,384]{0,1:T(8,128)(2,1)S(1)}, u32[]{:S(2)}, u32[]{:S(2)}) collective-permute-start(bf16[272,384]{0,1:T(8,128)(2,1)S(1)} %get-tuple-element.33), channel_id=1, source_target_pairs={{0,32},{16,48},{32,0},{48,16},{64,96},{80,112},{96,64},{112,80},{1... | collective-permute-start | bytes 626696 | tf_op jit(solution)/shard_map/cond/branch_1_fun/ppermute | solution.py:23
  27.2 85.2 %collective-permute-start.9 = (bf16[48,2560]{1,0:T(8,128)(2,1)}, bf16[48,2560]{1,0:T(8,128)(2,1)}, u32[]{:S(2)}, u32[]{:S(2)}) collective-permute-start(bf16[48,2560]{1,0:T(8,128)(2,1)} %constant_dynamic-slice_fusion.2), channel_id=1, source_target_pairs={{0,32},{16,48},{32,0},{48,16},{64,96},{80,112},{96,64},{112,80},{1... | collective-permute-start | bytes 737288 | tf_op jit(solution)/shard_map/cond/branch_1_fun/ppermute | solution.py:23
  31.9 52.8 %collective-permute-start.6 = (bf16[56,2560]{1,0:T(8,128)(2,1)S(1)}, bf16[56,2560]{1,0:T(8,128)(2,1)S(1)}, u32[]{:S(2)}, u32[]{:S(2)}) collective-permute-start(bf16[56,2560]{1,0:T(8,128)(2,1)S(1)} %get-tuple-element.32), channel_id=1, source_target_pairs={{0,32},{16,48},{32,0},{48,16},{64,96},{80,112},{96,64},{112,80},{1... | collective-permute-start | bytes 860168 | tf_op jit(solution)/shard_map/cond/branch_1_fun/ppermute | solution.py:23
  34.0 71.5 %collective-permute-start.8 = (bf16[56,2560]{1,0:T(8,128)(2,1)}, bf16[56,2560]{1,0:T(8,128)(2,1)}, u32[]{:S(2)}, u32[]{:S(2)}) collective-permute-start(bf16[56,2560]{1,0:T(8,128)(2,1)} %get-tuple-element.34), channel_id=1, source_target_pairs={{0,32},{16,48},{32,0},{48,16},{64,96},{80,112},{96,64},{112,80},{1... | collective-permute-start | bytes 860168 | tf_op jit(solution)/shard_map/cond/branch_1_fun/ppermute | solution.py:23
  38.7 77.8 %collective-permute-start.10 = (bf16[112,2560]{1,0:T(8,128)(2,1)}, bf16[112,2560]{1,0:T(8,128)(2,1)}, u32[]{:S(2)}, u32[]{:S(2)}) collective-permute-start(bf16[112,2560]{1,0:T(8,128)(2,1)} %slice.26), channel_id=1, source_target_pairs={{0,32},{16,48},{32,0},{48,16},{64,96},{80,112},{96,64},{112,80},{1... | collective-permute-start | bytes 1720328 | tf_op jit(solution)/shard_map/cond/branch_1_fun/ppermute | solution.py:23
  77.1 19.1 %collective-permute-start.5 = (f32[192,2560]{1,0:T(8,128)}, f32[192,2560]{1,0:T(8,128)}, u32[]{:S(2)}, u32[]{:S(2)}) collective-permute-start(f32[192,2560]{1,0:T(8,128)} %convolution_multiply_fusion.3), channel_id=1, source_target_pairs={{0,1},{1,0},{2,3},{3,2},{4,5},{5,4},{6,7},{7,6},{8,9},{9,8},{10,11... | collective-permute-start | bytes 5898248 | tf_op jit(solution)/shard_map/cond/branch_1_fun/ppermute | solution.py:27
  84.8 0.7 copy-start.20
  85.5 1.1 copy-start.10
  86.6 5.0 %copy-start.21 = (bf16[56,2560]{1,0:T(8,128)(2,1)S(1)}, bf16[56,2560]{1,0:T(8,128)(2,1)}, u32[]{:S(2)}) copy-start(bf16[56,2560]{1,0:T(8,128)(2,1)} %branch_1_fun.5) | copy-start | bytes 860164 | tf_op jit(solution)/shard_map/conditional
  90.0 9.7 %copy-start.5 = (f32[272,2560]{1,0:T(8,128)}, f32[272,2560]{1,0:T(8,128)S(1)}, u32[]{:S(2)}) copy-start(f32[272,2560]{1,0:T(8,128)S(1)} %fusion.29) | copy-start | bytes 8355844 | tf_op jit(solution)/shard_map/conditional
  90.0 3.3 %copy-start.2 = (bf16[432,2560]{1,0:T(8,128)(2,1)S(1)}, bf16[432,2560]{1,0:T(8,128)(2,1)}, u32[]{:S(2)}) copy-start(bf16[432,2560]{1,0:T(8,128)(2,1)} %get-tuple-element.31) | copy-start | bytes 6635524 | tf_op jit(solution)/shard_map/conditional
  90.0 6.1 %copy-start.14 = (bf16[8,1,24,432]{3,2,1,0:T(8,128)(2,1)S(1)}, bf16[8,1,24,432]{3,2,1,0:T(8,128)(2,1)}, u32[]{:S(2)}) copy-start(bf16[8,1,24,432]{3,2,1,0:T(8,128)(2,1)} %get-tuple-element.80) | copy-start | bytes 497668 | tf_op jit(solution)/shard_map/conditional
  94.2 32.8 %collective-permute-start.11 = (bf16[56,2560]{1,0:T(8,128)(2,1)}, bf16[56,2560]{1,0:T(8,128)(2,1)}, u32[]{:S(2)}, u32[]{:S(2)}) collective-permute-start(bf16[56,2560]{1,0:T(8,128)(2,1)} %get-tuple-element.65.refs_1_), channel_id=1, source_target_pairs={{0,32},{16,48},{32,0},{48,16},{64,96},{80,112},{96,64},{112,80},{1... | collective-permute-start | bytes 860168 | tf_op jit(solution)/shard_map/cond/branch_1_fun/ppermute | solution.py:23
  99.7 35.1 %all-to-all-start.1 = ((f32[8,24,2560]{2,1,0:T(8,128)}), f32[8,24,2560]{2,1,0:T(8,128)}, u32[]{:S(2)}, u32[]{:S(2)}) async-start(f32[8,24,2560]{2,1,0:T(8,128)} %bitcast.13.refs_2_), calls=%async_computation.1 | async-start | bytes 3932160 | tf_op jit(solution)/shard_map/cond/branch_1_fun/all_to_all | solution.py:33
  107.6 25.5 %collective-permute-start.12 = (bf16[56,2560]{1,0:T(8,128)(2,1)}, bf16[56,2560]{1,0:T(8,128)(2,1)}, u32[]{:S(2)}, u32[]{:S(2)}) collective-permute-start(bf16[56,2560]{1,0:T(8,128)(2,1)} %get-tuple-element.63.refs_1_), channel_id=1, source_target_pairs={{0,32},{16,48},{32,0},{48,16},{64,96},{80,112},{96,64},{112,80},{1... | collective-permute-start | bytes 860168 | tf_op jit(solution)/shard_map/cond/branch_1_fun/ppermute | solution.py:23
  114.6 22.6 %collective-permute-start.13 = (bf16[48,2560]{1,0:T(8,128)(2,1)}, bf16[48,2560]{1,0:T(8,128)(2,1)}, u32[]{:S(2)}, u32[]{:S(2)}) collective-permute-start(bf16[48,2560]{1,0:T(8,128)(2,1)} %get-tuple-element.61.refs_1_), channel_id=1, source_target_pairs={{0,32},{16,48},{32,0},{48,16},{64,96},{80,112},{96,64},{112,80},{1... | collective-permute-start | bytes 737288 | tf_op jit(solution)/shard_map/cond/branch_1_fun/ppermute | solution.py:23
Sparse Core Ops, SparseCore 0:
  21.4 47.7 all-gather.5

commit v3 on v2

--- a/solution.py
+++ b/solution.py
@@ -11,7 +11,7 @@
 HOP_LEVELS = 3
 SCALE = FF ** (-0.5)
 CORES = 2
-PLANS = {1: (112, (56, 56, 48), 1), 2: (0, (56, 56, 56, 48), 2)}
+PLANS = {1: (112, (56, 56, 48), 1), 2: (48, (56, 48, 48, 40), 2)}
 
 
 def after(value, *others):
@@ -118,19 +118,21 @@
             [flipped[:shared], lax.dynamic_slice_in_dim(flipped, first, half, 0)], 0
         )
 
-    far_flipped = trade(after(with_shared(other), shards), level)
+    late_weights = after(weights, shards) if level > 1 else weights
+    sent = with_shared(other)
+    far_flipped = trade(after(sent, shards) if level > 1 else sent, level)
     far_weights = [
-        trade(after(lax.dynamic_slice_in_dim(weights, other + a, n, 0), shards), level)
+        trade(after(lax.dynamic_slice_in_dim(late_weights, other + a, n, 0), shards), level)
         for a, n in pieces_of(pieces)
     ]
     if shared:
-        far_shared = trade(after(weights[:shared], shards), level)
+        far_shared = trade(after(late_weights[:shared], shards), level)
     both = lax.all_gather(shards, "tp", axis=0, tiled=True)
     chip_sum = chip_output(weights, after(hidden, both))
     layer_out = between_chips(chip_sum).sum(0).astype(jnp.bfloat16)
     paired = interleave(with_shared(mine), far_flipped, members)
     gradient = jnp.dot(paired, both, preferred_element_type=jnp.float32)
-    new_weights = jnp.zeros_like(weights)
+    new_weights = arrived(jnp.zeros_like(weights), shards, ahead=0)
     returned, order = [], []
     for k, ((a, n), far) in enumerate(zip(pieces_of(pieces), far_weights)):
         if k == forward_by:

time: 147 us -> 259 us (1.76)
  the two profiles are of different devices: /device:TPU:24 before, /device:TPU:1 now
where the time goes in v3:
time: 259 us; the launch traced here: 258 us
  waiting for transfers between devices  136 us (53%)
  starting transfers between devices  68.5 us (26%)
  local copies, waits for them, and re-layouts  19 us (7%)
  between operations  14.7 us (6%)
  other arithmetic  13.2 us (5%)
  matrix products  6.69 us (3%)
    ppermute x11, waiting for transfers between devices, trade(): return lax.ppermute(value, 'node', pairs)  133 us
    ppermute x11, starting transfers between devices, trade(): return lax.ppermute(value, 'node', pairs)  56.6 us
    dynamic_update_slice x4, other arithmetic, mixed_step(): lax.dynamic_update_slice_in_dim(new_weights, mean, mine + a, 0)  7.18 us
    another operation x26, local copies, waits for them, and re-layouts  7.03 us
    ppermute x1, starting transfers between devices, swap_cores(): lax.ppermute(value, 'tp', [(i, i ^ 1) for i in range(lax.axis_size('tp'))])  6.87 us
    dynamic_update_slice x4, local copies, waits for them, and re-layouts, mixed_step(): lax.dynamic_update_slice_in_dim(new_weights, mean, other + a, 0)  6.62 us
    dot_general x2, matrix products, partial_of(): jnp.dot(chosen.reshape(chips * shard, rows), weights, preferred_element_t...  5.55 us
  transfers between devices with their start and end apart: 14, of which 4 were waited for; matrix products, arithmetic and copies ran while one was open for 12% of the time, Pallas kernels for 0%

profile of v3, /device:TPU:1, one launch (start us, length us, event | category | flops | bytes accessed | tf_op | source)
XLA Modules:
  0.0 258.2 jit_solution(13782985450167633255)
XLA Ops:
  7.8 1.1 copy.28
  9.0 242.4 %conditional.2 = (bf16[24,2560]{1,0:T(8,128)(2,1)}, bf16[1,432,2560]{2,1,0:T(8,128)(2,1)}) conditional(s32[]{:T(128)} %bitcast.52, (bf16[1,384,432]{1,2,0:T(8,128)(2,1)}, bf16[432,2560]{1,0:T(8,128)(2,1)}, bf16[384,432]{1,0:T(8,128)(2,1)S(1)}, bf16[24,2560]{1,0:T(8,128)(2,1)}) %tuple.77, (bf16[24,2560]{1,0:T(8,128)(2,1)}, ...), branch_computations={%region_0.2_spmd, %region_2.4_spmd, %region_4.6_spmd} | conditional | flops 5001800318976 | bytes 133064272
  9.1 9.8 %collective-permute-start.14 = (bf16[24,2560]{1,0:T(8,128)(2,1)}, bf16[24,2560]{1,0:T(8,128)(2,1)}, u32[]{:S(2)}, u32[]{:S(2)}) collective-permute-start(bf16[24,2560]{1,0:T(8,128)(2,1)} %get-tuple-element.37), channel_id=1, source_target_pairs={{0,64},{16,80},{32,96},{48,112},{64,0},{80,16},{96,32},{112,48},{1... | collective-permute-start | bytes 368648 | tf_op jit(solution)/shard_map/cond/branch_2_fun/ppermute | solution.py:23
  24.5 7.7 %collective-permute-start.20 = (bf16[40,2560]{1,0:T(8,128)(2,1)}, bf16[40,2560]{1,0:T(8,128)(2,1)}, u32[]{:S(2)}, u32[]{:S(2)}) collective-permute-start(bf16[40,2560]{1,0:T(8,128)(2,1)} %constant_dynamic-slice_fusion.7), channel_id=1, source_target_pairs={{0,64},{16,80},{32,96},{48,112},{64,0},{80,16},{96,32},{112,48},{1... | collective-permute-start | bytes 614408 | tf_op jit(solution)/shard_map/cond/branch_2_fun/ppermute | solution.py:23
  32.3 1.9 collective-permute-start.16
  34.2 7.3 %collective-permute-start.17 = (bf16[240,384]{0,1:T(8,128)(2,1)}, bf16[240,384]{0,1:T(8,128)(2,1)S(1)}, u32[]{:S(2)}, u32[]{:S(2)}) collective-permute-start(bf16[240,384]{0,1:T(8,128)(2,1)} %get-tuple-element.42), channel_id=1, source_target_pairs={{0,64},{16,80},{32,96},{48,112},{64,0},{80,16},{96,32},{112,48},{1... | collective-permute-start | bytes 552968 | tf_op jit(solution)/shard_map/cond/branch_2_fun/ppermute | solution.py:23
  42.4 1.9 collective-permute-start.18
  44.3 7.3 %collective-permute-start.19 = (bf16[48,2560]{1,0:T(8,128)(2,1)}, bf16[48,2560]{1,0:T(8,128)(2,1)}, u32[]{:S(2)}, u32[]{:S(2)}) collective-permute-start(bf16[48,2560]{1,0:T(8,128)(2,1)} %get-tuple-element.44), channel_id=1, source_target_pairs={{0,64},{16,80},{32,96},{48,112},{64,0},{80,16},{96,32},{112,48},{1... | collective-permute-start | bytes 737288 | tf_op jit(solution)/shard_map/cond/branch_2_fun/ppermute | solution.py:23
  51.6 1.5 broadcast_36_refs_0_.0.refs_0_
  53.1 126.4 %collective-permute-done.17 = bf16[240,384]{0,1:T(8,128)(2,1)S(1)} collective-permute-done((bf16[240,384]{0,1:T(8,128)(2,1)}, bf16[240,384]{0,1:T(8,128)(2,1)S(1)}, u32[]{:S(2)}, u32[]{:S(2)}) %collective-permute-start.17) | collective-permute-done | bytes 184352 | tf_op jit(solution)/shard_map/cond/branch_2_fun/ppermute | solution.py:23
  179.5 2.1 collective-permute-start.21
  184.9 2.0 convolution_multiply_fusion.5
  186.9 6.9 %collective-permute-start.15 = (f32[192,2560]{1,0:T(8,128)}, f32[192,2560]{1,0:T(8,128)}, u32[]{:S(2)}, u32[]{:S(2)}) collective-permute-start(f32[192,2560]{1,0:T(8,128)} %convolution_multiply_fusion.5), channel_id=1, source_target_pairs={{0,1},{1,0},{2,3},{3,2},{4,5},{5,4},{6,7},{7,6},{8,9},{9,8},{10,11... | collective-permute-start | bytes 5898248 | tf_op jit(solution)/shard_map/cond/branch_2_fun/ppermute | solution.py:27
  193.8 1.1 fusion.35
  196.5 7.5 %collective-permute-start.22 = (bf16[56,2560]{1,0:T(8,128)(2,1)}, bf16[56,2560]{1,0:T(8,128)(2,1)}, u32[]{:S(2)}, u32[]{:S(2)}) collective-permute-start(bf16[56,2560]{1,0:T(8,128)(2,1)} %get-tuple-element.74.refs_1_), channel_id=1, source_target_pairs={{0,64},{16,80},{32,96},{48,112},{64,0},{80,16},{96,32},{112,48},{1... | collective-permute-start | bytes 860168 | tf_op jit(solution)/shard_map/cond/branch_2_fun/ppermute | solution.py:23
  204.1 1.6 copy-done.5
  205.7 2.0 bitcast_dynamic-update-slice_fusion.11
  207.7 1.9 collective-permute-start.23
  209.6 3.5 %fusion.13 = f32[192,2560]{1,0:T(8,128)} fusion(f32[192,2560]{1,0:T(8,128)} %collective-permute-done.15, bf16[192,432]{1,0:T(8,128)(2,1)S(1)} %bitcast.129, bf16[432,2560]{1,0:T(8,128)(2,1)S(1)} %copy-done.5), kind=kOutput, calls=%fused_computation.47 | convolution fusion | flops 425656320 | bytes 6309888 | tf_op jit(solution)/shard_map/cond/branch_2_fun/dot_general | solution.py:45
  213.2 5.0 %all-to-all-start.2 = ((f32[8,24,2560]{2,1,0:T(8,128)}), f32[8,24,2560]{2,1,0:T(8,128)}, u32[]{:S(2)}, u32[]{:S(2)}) async-start(f32[8,24,2560]{2,1,0:T(8,128)} %bitcast.118), calls=%async_computation.2 | async-start | bytes 3932160 | tf_op jit(solution)/shard_map/cond/branch_2_fun/all_to_all | solution.py:33
  218.2 2.1 bitcast_dynamic-update-slice_fusion.10
  220.3 7.3 %collective-permute-start.24 = (bf16[48,2560]{1,0:T(8,128)(2,1)}, bf16[48,2560]{1,0:T(8,128)(2,1)}, u32[]{:S(2)}, u32[]{:S(2)}) collective-permute-start(bf16[48,2560]{1,0:T(8,128)(2,1)} %get-tuple-element.70.refs_1_), channel_id=1, source_target_pairs={{0,64},{16,80},{32,96},{48,112},{64,0},{80,16},{96,32},{112,48},{1... | collective-permute-start | bytes 737288 | tf_op jit(solution)/shard_map/cond/branch_2_fun/ppermute | solution.py:23
  227.6 2.0 bitcast_dynamic-update-slice_fusion.13
  229.6 1.9 collective-permute-start.25
  231.6 2.0 fusion.25
  233.6 1.7 bitcast_dynamic-update-slice_fusion.6
  235.3 1.7 bitcast_dynamic-update-slice_fusion.9
  236.9 6.1 %collective-permute-done.24 = bf16[48,2560]{1,0:T(8,128)(2,1)} collective-permute-done((bf16[48,2560]{1,0:T(8,128)(2,1)}, bf16[48,2560]{1,0:T(8,128)(2,1)}, u32[]{:S(2)}, u32[]{:S(2)}) %collective-permute-start.24) | collective-permute-done | bytes 245792 | tf_op jit(solution)/shard_map/cond/branch_2_fun/ppermute | solution.py:23
  243.0 1.7 bitcast_dynamic-update-slice_fusion.8
  244.7 2.7 %all-to-all-done.2 = f32[8,24,2560]{2,1,0:T(8,128)} async-done(((f32[8,24,2560]{2,1,0:T(8,128)}), f32[8,24,2560]{2,1,0:T(8,128)}, u32[]{:S(2)}, u32[]{:S(2)}) %all-to-all-start.2) | async-done | bytes 1966112 | tf_op jit(solution)/shard_map/cond/branch_2_fun/all_to_all | solution.py:33
  247.4 2.3 reduce_sum.26.refs_1_
  249.8 1.6 bitcast_dynamic-update-slice_fusion.12
  (54 shorter events, 11.5 us)
Async XLA Ops:
  9.0 33.4 %copy-start.6 = (bf16[384,432]{1,0:T(8,128)(2,1)}, bf16[384,432]{1,0:T(8,128)(2,1)S(1)}, u32[]{:S(2)}) copy-start(bf16[384,432]{1,0:T(8,128)(2,1)S(1)} %get-tuple-element.38) | copy-start | bytes 995332 | tf_op jit(solution)/shard_map/conditional
  9.0 14.1 %copy-start.3 = (bf16[432,2560]{1,0:T(8,128)(2,1)S(1)}, bf16[432,2560]{1,0:T(8,128)(2,1)}, u32[]{:S(2)}) copy-start(bf16[432,2560]{1,0:T(8,128)(2,1)} %get-tuple-element.40) | copy-start | bytes 6635524 | tf_op jit(solution)/shard_map/conditional
  9.0 174.1 %all-gather.8.cloned.1.call-start = ((), (), s32[]{:S(2)}) async-start(), calls=%async_computation.5 | async-start | bytes 4177920 | tf_op jit(solution)/shard_map/cond/branch_2_fun/all_gather | solution.py:130
  9.1 12.4 %collective-permute-start.14 = (bf16[24,2560]{1,0:T(8,128)(2,1)}, bf16[24,2560]{1,0:T(8,128)(2,1)}, u32[]{:S(2)}, u32[]{:S(2)}) collective-permute-start(bf16[24,2560]{1,0:T(8,128)(2,1)} %get-tuple-element.37), channel_id=1, source_target_pairs={{0,64},{16,80},{32,96},{48,112},{64,0},{80,16},{96,32},{112,48},{1... | collective-permute-start | bytes 368648 | tf_op jit(solution)/shard_map/cond/branch_2_fun/ppermute | solution.py:23
  22.3 0.7 copy-start.13
  24.5 203.1 %collective-permute-start.20 = (bf16[40,2560]{1,0:T(8,128)(2,1)}, bf16[40,2560]{1,0:T(8,128)(2,1)}, u32[]{:S(2)}, u32[]{:S(2)}) collective-permute-start(bf16[40,2560]{1,0:T(8,128)(2,1)} %constant_dynamic-slice_fusion.7), channel_id=1, source_target_pairs={{0,64},{16,80},{32,96},{48,112},{64,0},{80,16},{96,32},{112,48},{1... | collective-permute-start | bytes 614408 | tf_op jit(solution)/shard_map/cond/branch_2_fun/ppermute | solution.py:23
  32.3 150.1 %collective-permute-start.16 = (bf16[56,2560]{1,0:T(8,128)(2,1)}, bf16[56,2560]{1,0:T(8,128)(2,1)S(1)}, u32[]{:S(2)}, u32[]{:S(2)}) collective-permute-start(bf16[56,2560]{1,0:T(8,128)(2,1)} %constant_dynamic-slice_fusion.10), channel_id=1, source_target_pairs={{0,64},{16,80},{32,96},{48,112},{64,0},{80,16},{96,32},{112,48},{1... | collective-permute-start | bytes 860168 | tf_op jit(solution)/shard_map/cond/branch_2_fun/ppermute | solution.py:23
  34.2 145.3 %collective-permute-start.17 = (bf16[240,384]{0,1:T(8,128)(2,1)}, bf16[240,384]{0,1:T(8,128)(2,1)S(1)}, u32[]{:S(2)}, u32[]{:S(2)}) collective-permute-start(bf16[240,384]{0,1:T(8,128)(2,1)} %get-tuple-element.42), channel_id=1, source_target_pairs={{0,64},{16,80},{32,96},{48,112},{64,0},{80,16},{96,32},{112,48},{1... | collective-permute-start | bytes 552968 | tf_op jit(solution)/shard_map/cond/branch_2_fun/ppermute | solution.py:23
  42.4 153.7 %collective-permute-start.18 = (bf16[48,2560]{1,0:T(8,128)(2,1)}, bf16[48,2560]{1,0:T(8,128)(2,1)}, u32[]{:S(2)}, u32[]{:S(2)}) collective-permute-start(bf16[48,2560]{1,0:T(8,128)(2,1)} %get-tuple-element.43), channel_id=1, source_target_pairs={{0,64},{16,80},{32,96},{48,112},{64,0},{80,16},{96,32},{112,48},{1... | collective-permute-start | bytes 737288 | tf_op jit(solution)/shard_map/cond/branch_2_fun/ppermute | solution.py:23
  44.3 173.9 %collective-permute-start.19 = (bf16[48,2560]{1,0:T(8,128)(2,1)}, bf16[48,2560]{1,0:T(8,128)(2,1)}, u32[]{:S(2)}, u32[]{:S(2)}) collective-permute-start(bf16[48,2560]{1,0:T(8,128)(2,1)} %get-tuple-element.44), channel_id=1, source_target_pairs={{0,64},{16,80},{32,96},{48,112},{64,0},{80,16},{96,32},{112,48},{1... | collective-permute-start | bytes 737288 | tf_op jit(solution)/shard_map/cond/branch_2_fun/ppermute | solution.py:23
  179.5 52.1 %collective-permute-start.21 = (bf16[48,2560]{1,0:T(8,128)(2,1)}, bf16[48,2560]{1,0:T(8,128)(2,1)}, u32[]{:S(2)}, u32[]{:S(2)}) collective-permute-start(bf16[48,2560]{1,0:T(8,128)(2,1)} %get-tuple-element.46), channel_id=1, source_target_pairs={{0,64},{16,80},{32,96},{48,112},{64,0},{80,16},{96,32},{112,48},{1... | collective-permute-start | bytes 737288 | tf_op jit(solution)/shard_map/cond/branch_2_fun/ppermute | solution.py:23
  182.4 0.7 copy-start.18
  183.1 1.0 copy-start.7
  183.1 1.8 copy-start.4
  184.8 8.9 %copy-start.10 = (bf16[768,2560]{1,0:T(8,128)(2,1)S(1)}, bf16[768,2560]{1,0:T(8,128)(2,1)}, u32[]{:S(2)}) copy-start(bf16[768,2560]{1,0:T(8,128)(2,1)} %all-gather.8.cloned.1.call-done) | copy-start | bytes 11796484 | tf_op jit(solution)/shard_map/conditional
  184.8 9.0 %copy-start.12 = (bf16[240,16,2,24]{0,3,2,1:T(8,128)(2,1)S(1)}, bf16[240,16,2,24]{0,3,2,1:T(8,128)(2,1)}, u32[]{:S(2)}) copy-start(bf16[240,16,2,24]{0,3,2,1:T(8,128)(2,1)} %pad_maximum_fusion.5) | copy-start | bytes 1105924 | tf_op jit(solution)/shard_map/conditional
  186.9 20.8 %collective-permute-start.15 = (f32[192,2560]{1,0:T(8,128)}, f32[192,2560]{1,0:T(8,128)}, u32[]{:S(2)}, u32[]{:S(2)}) collective-permute-start(f32[192,2560]{1,0:T(8,128)} %convolution_multiply_fusion.5), channel_id=1, source_target_pairs={{0,1},{1,0},{2,3},{3,2},{4,5},{5,4},{6,7},{7,6},{8,9},{9,8},{10,11... | collective-permute-start | bytes 5898248 | tf_op jit(solution)/shard_map/cond/branch_2_fun/ppermute | solution.py:27
  193.8 1.2 copy-start.19
  194.9 1.6 copy-start.9
  196.5 37.0 %collective-permute-start.22 = (bf16[56,2560]{1,0:T(8,128)(2,1)}, bf16[56,2560]{1,0:T(8,128)(2,1)}, u32[]{:S(2)}, u32[]{:S(2)}) collective-permute-start(bf16[56,2560]{1,0:T(8,128)(2,1)} %get-tuple-element.74.refs_1_), channel_id=1, source_target_pairs={{0,64},{16,80},{32,96},{48,112},{64,0},{80,16},{96,32},{112,48},{1... | collective-permute-start | bytes 860168 | tf_op jit(solution)/shard_map/cond/branch_2_fun/ppermute | solution.py:23
  204.1 1.6 copy-start.5
  204.1 5.5 %copy-start.15 = (bf16[8,1,24,432]{3,2,1,0:T(8,128)(2,1)S(1)}, bf16[8,1,24,432]{3,2,1,0:T(8,128)(2,1)}, u32[]{:S(2)}) copy-start(bf16[8,1,24,432]{3,2,1,0:T(8,128)(2,1)} %get-tuple-element.90) | copy-start | bytes 497668 | tf_op jit(solution)/shard_map/conditional
  207.7 27.6 %collective-permute-start.23 = (bf16[48,2560]{1,0:T(8,128)(2,1)}, bf16[48,2560]{1,0:T(8,128)(2,1)}, u32[]{:S(2)}, u32[]{:S(2)}) collective-permute-start(bf16[48,2560]{1,0:T(8,128)(2,1)} %get-tuple-element.72.refs_1_), channel_id=1, source_target_pairs={{0,64},{16,80},{32,96},{48,112},{64,0},{80,16},{96,32},{112,48},{1... | collective-permute-start | bytes 737288 | tf_op jit(solution)/shard_map/cond/branch_2_fun/ppermute | solution.py:23
  213.2 34.3 %all-to-all-start.2 = ((f32[8,24,2560]{2,1,0:T(8,128)}), f32[8,24,2560]{2,1,0:T(8,128)}, u32[]{:S(2)}, u32[]{:S(2)}) async-start(f32[8,24,2560]{2,1,0:T(8,128)} %bitcast.118), calls=%async_computation.2 | async-start | bytes 3932160 | tf_op jit(solution)/shard_map/cond/branch_2_fun/all_to_all | solution.py:33
  220.3 22.7 %collective-permute-start.24 = (bf16[48,2560]{1,0:T(8,128)(2,1)}, bf16[48,2560]{1,0:T(8,128)(2,1)}, u32[]{:S(2)}, u32[]{:S(2)}) collective-permute-start(bf16[48,2560]{1,0:T(8,128)(2,1)} %get-tuple-element.70.refs_1_), channel_id=1, source_target_pairs={{0,64},{16,80},{32,96},{48,112},{64,0},{80,16},{96,32},{112,48},{1... | collective-permute-start | bytes 737288 | tf_op jit(solution)/shard_map/cond/branch_2_fun/ppermute | solution.py:23
  229.6 20.1 %collective-permute-start.25 = (bf16[40,2560]{1,0:T(8,128)(2,1)}, bf16[40,2560]{1,0:T(8,128)(2,1)}, u32[]{:S(2)}, u32[]{:S(2)}) collective-permute-start(bf16[40,2560]{1,0:T(8,128)(2,1)} %get-tuple-element.68.refs_1_), channel_id=1, source_target_pairs={{0,64},{16,80},{32,96},{48,112},{64,0},{80,16},{96,32},{112,48},{1... | collective-permute-start | bytes 614408 | tf_op jit(solution)/shard_map/cond/branch_2_fun/ppermute | solution.py:23
Sparse Core Ops, SparseCore 0:
  23.2 57.0 all-gather.7

commit v4 on v3

--- a/solution.py
+++ b/solution.py
@@ -4,6 +4,7 @@
 import jax.numpy as jnp
 from jax import lax
 from jax.experimental import pallas as pl
+from jax.experimental.layout import Layout, with_layout_constraint
 from jax.sharding import PartitionSpec as P
 
 FF = 6912
@@ -11,7 +12,7 @@
 HOP_LEVELS = 3
 SCALE = FF ** (-0.5)
 CORES = 2
-PLANS = {1: (112, (56, 56, 48), 1), 2: (48, (56, 48, 48, 40), 2)}
+PLANS = {1: (112, (48, 56, 56), 1), 2: (48, (56, 48, 48, 40), 2)}
 
 
 def after(value, *others):
@@ -84,10 +85,11 @@
     members = lax.axis_size("tp")
     far_cotangent = trade(cotangent, level)
     far_hidden = trade(hidden, level)
-    far_weights = trade(weights, level)
     shards = jnp.concatenate([cotangent, far_cotangent], 0)
     both = lax.all_gather(shards, "tp", axis=0, tiled=True)
     chip_sum = chip_output(weights, hidden)
+    far_weights = trade(weights, level)
+    chip_sum = arrived(chip_sum)
     layer_out = between_chips(chip_sum).sum(0).astype(jnp.bfloat16)
     both = arrived(both, far_weights, layer_out, ahead=0)
     blocks = (members, tokens // members, rows)
@@ -153,6 +155,7 @@
 
 
 def per_device(weights, hidden, cotangent, hop_index):
+    hidden = with_layout_constraint(hidden, Layout(major_to_minor=(0, 1, 2)))
     branches = [
         partial(mixed_step if level in PLANS else whole_step, level) for level in range(HOP_LEVELS)
     ]

time: 259 us -> 101 us (0.39)
  waiting for transfers between devices: 136 us -> 48.3 us
  starting transfers between devices: 68.5 us -> 20 us
  local copies, waits for them, and re-layouts: 19 us -> 1.2 us
  other arithmetic: 13.2 us -> 1.55 us
  matrix products: 6.69 us -> 14.4 us
    ppermute x11 -> x3, waiting for transfers between devices: 133 us -> 47.3 us  [trade(): return lax.ppermute(value, 'node', pairs)]
    ppermute x11 -> x3, starting transfers between devices: 56.6 us -> 7.41 us  [trade(): return lax.ppermute(value, 'node', pairs)]
    dynamic_update_slice x5 -> x0, other arithmetic: 9.21 us -> none  [the longest x4 7.18 us: mixed_step(): lax.dynamic_update_slice_in_dim(new_weights, mean, mine + a, 0)]
    another operation x26 -> x6, local copies, waits for them, and re-layouts: 7.03 us -> 0.01 us
    dynamic_update_slice x4 -> x0, local copies, waits for them, and re-layouts: 6.62 us -> none  [mixed_step(): lax.dynamic_update_slice_in_dim(new_weights, mean, other + a, 0)]
    dot_general x1, matrix products: 1.14 us -> 7.2 us  [whole_step(): lax.dot_general(panel.reshape(2 * tokens, rows), both, (((0,), (0,)), (()...]
    all_to_all x1, waiting for transfers between devices: 2.75 us -> 0.01 us  [between_chips(): lax.all_to_all(blocks, 'tp', 0, 0, axis_index_groups=same_core, tiled=True)]
  transfers between devices with their start and end apart: 14 -> 6, of which waited for: 4 -> 3; matrix products, arithmetic and copies ran while one was open for 12% -> 5% of each run, Pallas kernels for 0% -> 0%
where the time goes in v4:
time: 101 us; the launch traced here: 100 us
  waiting for transfers between devices  48.3 us (48%)
  starting transfers between devices  20 us (20%)
  between operations  14.7 us (15%)
  matrix products  14.4 us (14%)
  other arithmetic  1.55 us (2%)
  local copies, waits for them, and re-layouts  1.2 us (1%)
    ppermute x3, waiting for transfers between devices, trade(): return lax.ppermute(value, 'node', pairs)  47.3 us
    ppermute x1, starting transfers between devices, swap_cores(): lax.ppermute(value, 'tp', [(i, i ^ 1) for i in range(lax.axis_size('tp'))])  8.78 us
    ppermute x3, starting transfers between devices, trade(): return lax.ppermute(value, 'node', pairs)  7.41 us
    dot_general x2, matrix products, partial_of(): jnp.dot(chosen.reshape(chips * shard, rows), weights, preferred_element_t...  7.21 us
    dot_general x1, matrix products, whole_step(): lax.dot_general(panel.reshape(2 * tokens, rows), both, (((0,), (0,)), (()...  7.2 us
    all_to_all x1, starting transfers between devices, between_chips(): lax.all_to_all(blocks, 'tp', 0, 0, axis_index_groups=same_core, tiled=True)  3.73 us
  transfers between devices with their start and end apart: 6, of which 3 were waited for; matrix products, arithmetic and copies ran while one was open for 5% of the time, Pallas kernels for 0%

profile of v4, /device:TPU:1, one launch (start us, length us, event | category | flops | bytes accessed | tf_op | source)
XLA Modules:
  0.0 100.2 jit_solution(1574647113999611674)
XLA Ops:
  7.8 1.1 %copy.28 = bf16[1,384,432]{2,1,0:T(8,128)(2,1)S(1)} copy(bf16[1,384,432]{1,2,0:T(8,128)(2,1)} %param.8) | data formatting | bytes 663552 | tf_op args[1]
  9.0 84.4 %conditional.2 = (bf16[24,2560]{1,0:T(8,128)(2,1)}, bf16[1,432,2560]{2,1,0:T(8,128)(2,1)}) conditional(s32[]{:T(128)} %bitcast.52, (bf16[1,384,432]{2,1,0:T(8,128)(2,1)S(1)}, bf16[432,2560]{1,0:T(8,128)(2,1)}, bf16[384,432]{1,0:T(8,128)(2,1)S(1)}, bf16[24,2560]{1,0:T(8,128)(2,1)}) %tuple.72, (bf16[24,2560]{1,0:T(8,128)(2,1)}, ...), branch_computations={%region_0.2_spmd, %region_2.4_spmd, %region_4.6_spmd} | conditional | flops 5001800318976 | bytes 106522112
  9.0 0.0 copy-start
  9.0 0.0 all-gather.4.cloned.1.call-start
  9.1 0.0 copy-start.11
  9.1 3.6 %convolution_multiply_fusion.1 = f32[192,2560]{1,0:T(8,128)} fusion(bf16[192,432]{1,0:T(8,128)(2,1)S(1)} %bitcast.127, bf16[432,2560]{1,0:T(8,128)(2,1)} %get-tuple-element.25), kind=kOutput, calls=%fused_computation.2 | convolution fusion | flops 425164800 | bytes 4343808 | tf_op jit(solution)/shard_map/cond/branch_0_fun/dot_general | solution.py:46
  12.7 0.0 copy-done
  12.7 8.8 %collective-permute-start = (f32[192,2560]{1,0:T(8,128)}, f32[192,2560]{1,0:T(8,128)S(1)}, u32[]{:S(2)}, u32[]{:S(2)}) collective-permute-start(f32[192,2560]{1,0:T(8,128)} %convolution_multiply_fusion.1), channel_id=1, source_target_pairs={{0,1},{1,0},{2,3},{3,2},{4,5},{5,4},{6,7},{7,6},{8,9},{9,8},{10,11... | collective-permute-start | bytes 5898248 | tf_op jit(solution)/shard_map/cond/branch_0_fun/ppermute | solution.py:28
  21.5 0.0 copy-done.11
  21.5 1.9 %collective-permute-start.3 = (bf16[24,2560]{1,0:T(8,128)(2,1)S(1)}, bf16[24,2560]{1,0:T(8,128)(2,1)S(1)}, u32[]{:S(2)}, u32[]{:S(2)}) collective-permute-start(bf16[24,2560]{1,0:T(8,128)(2,1)S(1)} %copy-done.11), channel_id=1, source_target_pairs={{0,16},{16,0},{32,48},{48,32},{64,80},{80,64},{96,112},{112,96},{1... | collective-permute-start | bytes 368648 | tf_op jit(solution)/shard_map/cond/branch_0_fun/ppermute | solution.py:24
  23.5 3.4 %collective-permute-start.1 = (bf16[432,2560]{1,0:T(8,128)(2,1)}, bf16[432,2560]{1,0:T(8,128)(2,1)}, u32[]{:S(2)}, u32[]{:S(2)}) collective-permute-start(bf16[432,2560]{1,0:T(8,128)(2,1)} %get-tuple-element.25), channel_id=1, source_target_pairs={{0,16},{16,0},{32,48},{48,32},{64,80},{80,64},{96,112},{112,96},{1... | collective-permute-start | bytes 6635528 | tf_op jit(solution)/shard_map/cond/branch_0_fun/ppermute | solution.py:24
  26.8 1.5 %collective-permute-done.3 = bf16[24,2560]{1,0:T(8,128)(2,1)S(1)} collective-permute-done((bf16[24,2560]{1,0:T(8,128)(2,1)S(1)}, bf16[24,2560]{1,0:T(8,128)(2,1)S(1)}, u32[]{:S(2)}, u32[]{:S(2)}) %collective-permute-start.3) | collective-permute-done | bytes 122912 | tf_op jit(solution)/shard_map/cond/branch_0_fun/ppermute | solution.py:24
  28.4 0.7 pad_maximum_fusion.1
  29.1 0.0 all-gather.4.cloned.1.call-update
  29.1 0.0 collective-permute-done
  29.1 3.6 %fusion = f32[192,2560]{1,0:T(8,128)} fusion(f32[192,2560]{1,0:T(8,128)S(1)} %collective-permute-done, bf16[192,432]{1,0:T(8,128)(2,1)S(1)} %bitcast.125, bf16[432,2560]{1,0:T(8,128)(2,1)} %get-tuple-element.25), kind=kOutput, calls=%fused_computation.4 | convolution fusion | flops 425656320 | bytes 6309888 | tf_op jit(solution)/shard_map/cond/branch_0_fun/dot_general | solution.py:46
  32.7 0.0 copy-start.1
  32.7 3.7 %all-to-all-start = ((f32[8,24,2560]{2,1,0:T(8,128)}), f32[8,24,2560]{2,1,0:T(8,128)S(1)}, u32[]{:S(2)}, u32[]{:S(2)}) async-start(f32[8,24,2560]{2,1,0:T(8,128)} %branch_0_fun.2), calls=%async_computation | async-start | bytes 3932160 | tf_op jit(solution)/shard_map/cond/branch_0_fun/all_to_all | solution.py:34
  36.4 0.0 copy-done.1
  36.4 2.1 %collective-permute-start.2 = (bf16[384,432]{1,0:T(8,128)(2,1)S(1)}, bf16[384,432]{1,0:T(8,128)(2,1)S(1)}, u32[]{:S(2)}, u32[]{:S(2)}) collective-permute-start(bf16[384,432]{1,0:T(8,128)(2,1)S(1)} %copy-done.1), channel_id=1, source_target_pairs={{0,16},{16,0},{32,48},{48,32},{64,80},{80,64},{96,112},{112,96},{1... | collective-permute-start | bytes 995336 | tf_op jit(solution)/shard_map/cond/branch_0_fun/ppermute | solution.py:24
  38.6 45.7 %collective-permute-done.2 = bf16[384,432]{1,0:T(8,128)(2,1)S(1)} collective-permute-done((bf16[384,432]{1,0:T(8,128)(2,1)S(1)}, bf16[384,432]{1,0:T(8,128)(2,1)S(1)}, u32[]{:S(2)}, u32[]{:S(2)}) %collective-permute-start.2) | collective-permute-done | bytes 331808 | tf_op jit(solution)/shard_map/cond/branch_0_fun/ppermute | solution.py:24
  84.3 0.1 pad_maximum_fusion
  84.4 0.0 all-to-all-done
  84.4 0.8 reduce_sum.24.refs_2_
  85.2 0.0 collective-permute-done.1.refs_1_
  85.2 1.0 all-gather.4.cloned.1.call-done.refs_0_
  86.1 7.2 %fusion.1 = bf16[1,432,2560]{2,1,0:T(8,128)(2,1)} fusion(bf16[432,2560]{1,0:T(8,128)(2,1)} %collective-permute-done.1.refs_1_, bf16[432,2560]{1,0:T(8,128)(2,1)} %get-tuple-element.25, bf16[768,432]{1,0:T(8,128)(2,1)S(1)} %bitcast.130, bf16[768,2560]{1,0:T(8,128)(2,1)} %branch_0_fun.3), kind=kOutput, calls=%fused_computation.5 | convolution fusion | flops 1706434560 | bytes 11231232 | tf_op jit(solution)/shard_map/cond/branch_0_fun/dot_general | solution.py:97
  (3 shorter events, 0.0 us)
Async XLA Ops:
  9.0 3.8 %copy-start = (bf16[384,432]{1,0:T(8,128)(2,1)}, bf16[384,432]{1,0:T(8,128)(2,1)S(1)}, u32[]{:S(2)}) copy-start(bf16[384,432]{1,0:T(8,128)(2,1)S(1)} %get-tuple-element.26) | copy-start | bytes 995332 | tf_op jit(solution)/shard_map/conditional
  9.0 77.2 %all-gather.4.cloned.1.call-start = ((), (), s32[]{:S(2)}) async-start(), calls=%async_computation.3 | async-start | bytes 4177920 | tf_op jit(solution)/shard_map/cond/branch_0_fun/all_gather | solution.py:89
  9.1 12.4 %copy-start.11 = (bf16[24,2560]{1,0:T(8,128)(2,1)S(1)}, bf16[24,2560]{1,0:T(8,128)(2,1)}, u32[]{:S(2)}) copy-start(bf16[24,2560]{1,0:T(8,128)(2,1)} %get-tuple-element.27) | copy-start | bytes 368644 | tf_op jit(solution)/shard_map/conditional
  12.7 16.4 %collective-permute-start = (f32[192,2560]{1,0:T(8,128)}, f32[192,2560]{1,0:T(8,128)S(1)}, u32[]{:S(2)}, u32[]{:S(2)}) collective-permute-start(f32[192,2560]{1,0:T(8,128)} %convolution_multiply_fusion.1), channel_id=1, source_target_pairs={{0,1},{1,0},{2,3},{3,2},{4,5},{5,4},{6,7},{7,6},{8,9},{9,8},{10,11... | collective-permute-start | bytes 5898248 | tf_op jit(solution)/shard_map/cond/branch_0_fun/ppermute | solution.py:28
  21.5 6.8 %collective-permute-start.3 = (bf16[24,2560]{1,0:T(8,128)(2,1)S(1)}, bf16[24,2560]{1,0:T(8,128)(2,1)S(1)}, u32[]{:S(2)}, u32[]{:S(2)}) collective-permute-start(bf16[24,2560]{1,0:T(8,128)(2,1)S(1)} %copy-done.11), channel_id=1, source_target_pairs={{0,16},{16,0},{32,48},{48,32},{64,80},{80,64},{96,112},{112,96},{1... | collective-permute-start | bytes 368648 | tf_op jit(solution)/shard_map/cond/branch_0_fun/ppermute | solution.py:24
  23.5 61.7 %collective-permute-start.1 = (bf16[432,2560]{1,0:T(8,128)(2,1)}, bf16[432,2560]{1,0:T(8,128)(2,1)}, u32[]{:S(2)}, u32[]{:S(2)}) collective-permute-start(bf16[432,2560]{1,0:T(8,128)(2,1)} %get-tuple-element.25), channel_id=1, source_target_pairs={{0,16},{16,0},{32,48},{48,32},{64,80},{80,64},{96,112},{112,96},{1... | collective-permute-start | bytes 6635528 | tf_op jit(solution)/shard_map/cond/branch_0_fun/ppermute | solution.py:24
  32.7 3.7 %copy-start.1 = (bf16[384,432]{1,0:T(8,128)(2,1)S(1)}, bf16[384,432]{1,0:T(8,128)(2,1)}, u32[]{:S(2)}) copy-start(bf16[384,432]{1,0:T(8,128)(2,1)} %copy-done) | copy-start | bytes 995332 | tf_op jit(solution)/shard_map/conditional
  32.7 51.7 %all-to-all-start = ((f32[8,24,2560]{2,1,0:T(8,128)}), f32[8,24,2560]{2,1,0:T(8,128)S(1)}, u32[]{:S(2)}, u32[]{:S(2)}) async-start(f32[8,24,2560]{2,1,0:T(8,128)} %branch_0_fun.2), calls=%async_computation | async-start | bytes 3932160 | tf_op jit(solution)/shard_map/cond/branch_0_fun/all_to_all | solution.py:34
  36.4 47.9 %collective-permute-start.2 = (bf16[384,432]{1,0:T(8,128)(2,1)S(1)}, bf16[384,432]{1,0:T(8,128)(2,1)S(1)}, u32[]{:S(2)}, u32[]{:S(2)}) collective-permute-start(bf16[384,432]{1,0:T(8,128)(2,1)S(1)} %copy-done.1), channel_id=1, source_target_pairs={{0,16},{16,0},{32,48},{48,32},{64,80},{80,64},{96,112},{112,96},{1... | collective-permute-start | bytes 995336 | tf_op jit(solution)/shard_map/cond/branch_0_fun/ppermute | solution.py:24
Sparse Core Ops, SparseCore 0:
  29.2 56.8 all-gather.3
